TPU v7x, 128 devices: a whole 4x4x4 slice. The times are simulated.
128 devices in a mesh: gx: 4 (over y), gy: 32 (over z, x, core).
Axes of the slice: x: 4, y: 4, z: 4, core: 2. Of those that a mesh axis runs over, the one named last changes fastest.
Arguments:
- rhs: float32 [32, 256, 128], P('gy', 'gx'), may hold values from -6 to 6
- fine_blocks: float32 [32, 256, 3, 128, 128], P('gy', 'gx'), may hold values from -1 to 5
- smoother: float32 [32, 256, 128, 128], P('gy', 'gx'), may hold values from -0.1 to 0.3
- columns: int32 [32, 256, 3], P('gy', 'gx'), may hold values from 0 to 255, as said below
- aggregates: int32 [32, 256, 128], P('gy', 'gx'), may hold values from 0 to 16383, as said below
- weights: float32 [32, 256, 128], P('gy', 'gx'), may hold values from 0.1 to 0.3
- coarse_lower: float32 [128, 128, 128], P('gy'), may hold values from -1.2 to 0.3
- coarse_upper: float32 [128, 128, 128], P('gy'), may hold values from -1.2 to 0.3
- coarse_pivot: float32 [128, 128, 128], P('gy'), may hold values from -0.3 to 1.7
Outputs:
- solution_field: float32 [32, 256, 128], P('gy', 'gx')
- coarse_solution: float32 [128, 128], P('gy')
Inputs may be any that keep to these rules, and one draw needn't show every extreme that they name: `columns`: column 0 of each block row is the row itself; every other column lies within 2 blocks of the row in the same line. With g = (l * 256 + n) * 128 + b the fine row's index over all lines, aggregates[l, n, b] differs by at most 256 from g // 64; the first fine row takes 0 and the last 16383.
All inputs are finite; a program needn't handle non-finite values.
Results may differ from a plain program's by a relative error of at most 0.0003.
Values sent between devices are 32-bit elements; how exact they have to be, the bound alone decides.
No kernel may reach another device: no remote copies, remote signals or barrier semaphores. Data moves between devices by JAX's collectives and lax.ppermute only.
A program may use at most 128 MiB of HBM per device.

v0:
```python
import jax
import jax.numpy as jnp
from jax import lax
from jax.experimental import pallas as pl
from jax.experimental.pallas import tpu as pltpu
from jax.sharding import PartitionSpec as P

BS = 128
ROWS = 64
FEXT = ROWS + 8
CHUNK = 8
LOWER, UPPER, PIVOT, INSIDE = 0, 4, 8, 12
GROUPS = 32
f32 = jnp.float32
VMEM = pl.BlockSpec(memory_space=pltpu.VMEM)
SMEM = pl.BlockSpec(memory_space=pltpu.SMEM)
HBM = pl.BlockSpec(memory_space=pltpu.HBM)


def grant(mib):
    return pltpu.CompilerParams(vmem_limit_bytes=mib * 1024 * 1024)


def shape(*dims):
    return jax.ShapeDtypeStruct(dims, f32)


def identity_mask():
    rows = lax.broadcasted_iota(jnp.int32, (BS, BS), 0)
    columns = lax.broadcasted_iota(jnp.int32, (BS, BS), 1)
    return rows == columns


def column_to_row(column, eye):
    return jnp.sum(jnp.where(eye, column, 0.0), axis=0, keepdims=True)


def times_row(matrix, row, eye):
    return column_to_row(jnp.sum(matrix * row, axis=1, keepdims=True), eye)


def halves(value):
    high = value.astype(jnp.bfloat16)
    return high, (value - high.astype(f32)).astype(jnp.bfloat16)


def product(left, right):
    left_high, left_low = halves(left)
    right_high, right_low = halves(right)
    return jnp.dot(
        jnp.concatenate([left_high, left_high, left_low], axis=1),
        jnp.concatenate([right_high, right_low, right_high], axis=0),
        preferred_element_type=f32,
    )


def maps_kernel(lower, upper, pivot, maps_out, mine_out, maps, mine, sems, out_sems):
    coarse = [
        pltpu.make_async_copy(source, mine.at[pl.ds(4 * at, 4)], sems.at[at])
        for at, source in enumerate((lower, upper, pivot))
    ]
    for action in coarse:
        action.start()
    coarse[0].wait()
    forward = [-mine[LOWER]]
    for j in range(1, 4):
        forward.append(-product(mine[LOWER + j], forward[-1]))
    for action in coarse[1:]:
        action.wait()
    both = product(mine[PIVOT + 3], jnp.concatenate([forward[3], -mine[UPPER + 3]], axis=1))
    for j in (3, 2, 1, 0):
        if j < 3:
            both = product(mine[UPPER + j], both)
            both = product(mine[PIVOT + j], jnp.concatenate([forward[j] - both[:, :BS], -both[:, BS:]], axis=1))
        mine[INSIDE + 2 * j] = both[:, :BS]
        mine[INSIDE + 2 * j + 1] = both[:, BS:]
    odd = lax.axis_index("gy") % 2 == 1
    for at, value in enumerate((forward[3], both[:, :BS], both[:, BS:])):
        maps[at] = jnp.where(odd, value.T, value)
    sent = [
        pltpu.make_async_copy(maps, maps_out, out_sems.at[0]),
        pltpu.make_async_copy(mine, mine_out, out_sems.at[1]),
    ]
    for action in sent:
        action.start()
    for action in sent:
        action.wait()


def pack_kernel(
    rhs, weights, aggregates, columns, fine, smoother,
    to_previous, to_next,
    packed, edge, ends, indices, sems, out_sems,
):
    eye = identity_mask()

    def start(source, target, *at):
        action = pltpu.make_async_copy(source, target, sems.at[at])
        action.start()
        return action

    near, far = [], []
    for side in range(2):
        top = side * (ROWS - 8)
        near.append(start(smoother.at[pl.ds(side * (ROWS - 4), 4)], edge.at[side], side, 0))
        near.append(start(rhs.at[pl.ds(top, 8)], ends.at[side, 0], side, 1))
        near.append(start(weights.at[pl.ds(top, 8)], ends.at[side, 1], side, 2))
        near.append(start(aggregates.at[pl.ds(top, 8)], indices.at[side], side, 3))
    for side in range(2):
        far.append(start(fine.at[pl.ds(side * (ROWS - 2) * 3, 6)], packed.at[side, pl.ds(0, 6)], side, 4))
    for action in near:
        action.wait()
    lane = lax.broadcasted_iota(jnp.int32, (8, BS), 1)
    for side in range(2):
        top = 4 * side
        packed[side, 6] = edge[side, 2 * side].T
        packed[side, 7] = edge[side, 2 * side + 1].T
        for r in range(4):
            packed[side, 8, r : r + 1] = times_row(edge[side, r], ends[side, 0, top + r : top + r + 1], eye)
        packed[side, 8, 4:8] = ends[side, 1, top : top + 4]
        packed[side, 8, 8:12] = indices[side, top : top + 4].astype(f32)
        packed[side, 8, 12:16] = jnp.zeros((4, BS), f32)
        picked = jnp.zeros((8, BS), jnp.int32)
        for r in range(2):
            for k in range(3):
                picked = jnp.where(lane == 3 * r + k, columns[k, 0, side * (ROWS - 2) + r], picked)
        packed[side, 8, 16:24] = picked.astype(f32)
        packed[side, 8, 24:BS] = jnp.zeros((BS - 24, BS), f32)
    for action in far:
        action.wait()
    sent = [
        pltpu.make_async_copy(packed.at[side], target, out_sems.at[side])
        for side, target in enumerate((to_previous, to_next))
    ]
    for action in sent:
        action.start()
    for action in sent:
        action.wait()


def first_kernel(rhs, smoother, turned, first, smooth, rhs_rows, sems, rhs_sem):
    eye = identity_mask()
    n_chunks = ROWS // CHUNK

    def smooth_copy(c):
        rows = pl.ds(c * CHUNK, CHUNK)
        return pltpu.make_async_copy(smoother.at[rows], smooth.at[rows], sems.at[c])

    small = pltpu.make_async_copy(rhs, rhs_rows, rhs_sem)
    small.start()
    for c in range(n_chunks):
        smooth_copy(c).start()
    small.wait()
    for c in range(n_chunks):
        smooth_copy(c).wait()

        def row(r, _):
            n = c * CHUNK + r
            block = smooth[n]
            column = jnp.sum(block * rhs_rows[pl.ds(n, 1)], axis=1, keepdims=True)
            first[pl.ds(n, 1)] = column_to_row(column, eye)
            turned[n] = block.T
            return 0

        lax.fori_loop(0, CHUNK, row, 0, unroll=8)


def change_row(blocks, at, turned_block, source, picks):
    total = blocks[at] * source[pl.ds(picks[0], 1)]
    total += blocks[at + 1] * source[pl.ds(picks[1], 1)]
    total += blocks[at + 2] * source[pl.ds(picks[2], 1)]
    column = jnp.sum(total, axis=1, keepdims=True)
    if turned_block is None:
        return column
    return jnp.sum(turned_block * column, axis=0, keepdims=True)


def picks_of(columns, n, base):
    return [jnp.clip(columns[k, 0, n] - base, 0, FEXT - 1) for k in range(3)]


def halo_picks(halo_columns, side, r, base):
    return [
        jnp.clip(halo_columns[side, 0, 3 * r + k].astype(jnp.int32) - base, 0, FEXT - 1) for k in range(3)]


def presmooth_kernel(
    rhs, weights, aggregates, columns, fine, turned, first, before, after,
    shared, first_field, second_own,
    blocks, second_field, residual, rows, indices, halo_columns, sems, block_sems,
):
    gx = lax.axis_index("gx")
    gy = lax.axis_index("gy")
    eye = identity_mask()
    copies = [
        pltpu.make_async_copy(before.at[8, pl.ds(16, 8)], halo_columns.at[0], sems.at[0]),
        pltpu.make_async_copy(after.at[8, pl.ds(16, 8)], halo_columns.at[1], sems.at[1]),
        pltpu.make_async_copy(rhs, rows.at[0], sems.at[2]),
        pltpu.make_async_copy(weights, rows.at[1], sems.at[3]),
        pltpu.make_async_copy(aggregates, indices, sems.at[4]),
    ]
    n_chunks = ROWS // CHUNK

    def block_copy(c):
        part = pl.ds(c * CHUNK * 3, CHUNK * 3)
        return pltpu.make_async_copy(fine.at[part], blocks.at[part], block_sems.at[c])

    for c in range(n_chunks):
        block_copy(c).start()
    for action in copies:
        action.start()
    base = gx * ROWS - 4
    first_field[4 : ROWS + 4] = first[...]
    first_field[0:4] = before[8, 0:4]
    first_field[FEXT - 4 : FEXT] = after[8, 0:4]
    second_field[0:2] = jnp.zeros((2, BS), f32)
    second_field[FEXT - 2 : FEXT] = jnp.zeros((2, BS), f32)

    def second_row(n, _):
        change = change_row(blocks, 3 * n, turned[n], first_field, picks_of(columns, n, base))
        second_field[pl.ds(n + 4, 1)] = 2.0 * first_field[pl.ds(n + 4, 1)] - change
        return 0

    for c in range(n_chunks):
        block_copy(c).wait()
        lax.fori_loop(c * CHUNK, c * CHUNK + CHUNK, second_row, 0, unroll=8)
    copies[0].wait()
    copies[1].wait()
    for side, source in ((0, before), (1, after)):
        for r in range(2):
            at = side * (ROWS + 2) + 2 + r
            change = change_row(
                source, 3 * r, source[6 + r], first_field, halo_picks(halo_columns, side, r, base))
            second_field[at : at + 1] = 2.0 * first_field[at : at + 1] - change
    second_own[...] = second_field[4 : ROWS + 4]

    def residual_row(n, _):
        column = change_row(blocks, 3 * n, None, second_field, picks_of(columns, n, base))
        residual[pl.ds(n, 1)] = column_to_row(column, eye)
        return 0

    lax.fori_loop(0, ROWS, residual_row, 0, unroll=8)
    for action in copies[2:]:
        action.wait()
    residual[...] = rows[1] * (rows[0] - residual[...])
    low_block = gy * 4 - 2
    row8 = lax.broadcasted_iota(jnp.int32, (8, BS), 0)
    row128 = lax.broadcasted_iota(jnp.int32, (BS, BS), 0)

    def scatter(n, total):
        index = indices[pl.ds(n, 1)]
        block, within = (index >> 7) - low_block, index & 127
        value = jnp.where(row8 == block, residual[pl.ds(n, 1)], 0.0)
        high = value.astype(jnp.bfloat16).astype(f32)
        parts = jnp.concatenate([high, value - high], axis=0).astype(jnp.bfloat16)
        hot = jnp.where(row128 == within, 1.0, 0.0).astype(jnp.bfloat16)
        return total + lax.dot_general(parts, hot, (((1,), (1,)), ((), ())), preferred_element_type=f32)

    total = lax.fori_loop(0, ROWS, scatter, jnp.zeros((16, BS), f32), unroll=8)
    shared[0:8] = total[0:8] + total[8:16]
    shared[8:40] = jnp.zeros((32, BS), f32)
    shared[pl.ds(pl.multiple_of(8 + 8 * gx, 8), 8)] = jnp.concatenate(
        [second_field[4:8], second_field[FEXT - 8 : FEXT - 4]], axis=0)


def local_kernel(shared, mine, previous, following, out):
    eye = identity_mask()
    zero = jnp.zeros((1, BS), f32)
    own = [shared[j : j + 1] for j in range(8)]
    groups = (
        (previous, [zero, zero, own[0], own[1]]),
        (mine, own[2:6]),
        (following, [own[6], own[7], zero, zero]),
    )
    inner = [[right[0]] for _, right in groups]
    for j in range(1, 4):
        for (source, right), found in zip(groups, inner):
            found.append(right[j] - times_row(source[LOWER + j], found[-1], eye))
    solved = [[None] * 4 for _ in groups]
    for j in (3, 2, 1, 0):
        held = []
        for (source, _), found, x in zip(groups, inner, solved):
            held.append(found[j] if j == 3 else found[j] - times_row(source[UPPER + j], x[j + 1], eye))
        for (source, _), value, x in zip(groups, held, solved):
            x[j] = times_row(source[PIVOT + j], value, eye)
    tiles = []
    for found, x in zip(inner, solved):
        tiles += x + [found[3], zero, zero, zero]
    tile = jnp.concatenate(tiles, axis=0)
    for peer in range(GROUPS):
        out[peer] = tile


def correct_kernel(
    parts_hbm, shared, first_field, second_own, weights, aggregates, columns, maps, mine, previous, following,
    fine, turned_hbm, before_hbm, after_hbm,
    field_out, coarse_out,
    parts, chain, inside, blocks, turned, halo, sums, entering, leaving, window, field, next_field, halo_columns,
    weight_rows, indices, sems, chain_sems, block_sems,
):
    gx = lax.axis_index("gx")
    gy = lax.axis_index("gy")
    eye = identity_mask()
    step = 8
    chain_copies = {}
    arrived = pltpu.make_async_copy(parts_hbm, parts, sems.at[4])
    arrived.start()
    for kind in (0, 1, 2):
        order = range(GROUPS // step) if kind < 2 else reversed(range(GROUPS // step))
        for c in order:
            action = pltpu.make_async_copy(
                maps.at[pl.ds(c * step, step), kind], chain.at[kind, pl.ds(c * step, step)], chain_sems.at[kind, c])
            action.start()
            chain_copies[kind, c] = action
    copies = [
        pltpu.make_async_copy(previous.at[pl.ds(INSIDE + 4, 4)], inside.at[pl.ds(0, 4)], sems.at[5]),
        pltpu.make_async_copy(mine.at[pl.ds(INSIDE, 8)], inside.at[pl.ds(4, 8)], sems.at[6]),
        pltpu.make_async_copy(following.at[pl.ds(INSIDE, 4)], inside.at[pl.ds(12, 4)], sems.at[7]),
        pltpu.make_async_copy(before_hbm.at[8, pl.ds(16, 8)], halo_columns.at[0], sems.at[0]),
        pltpu.make_async_copy(after_hbm.at[8, pl.ds(16, 8)], halo_columns.at[1], sems.at[1]),
        pltpu.make_async_copy(weights, weight_rows, sems.at[2]),
        pltpu.make_async_copy(aggregates, indices, sems.at[3]),
        pltpu.make_async_copy(before_hbm, halo.at[0], sems.at[8]),
        pltpu.make_async_copy(after_hbm, halo.at[1], sems.at[9]),
    ]
    for action in copies:
        action.start()
    whole = [pltpu.make_async_copy(turned_hbm, turned, sems.at[10])]
    for c in range(4):
        rows = pl.ds(c * (ROWS * 3 // 4), ROWS * 3 // 4)
        whole.append(pltpu.make_async_copy(fine.at[rows], blocks.at[rows], block_sems.at[c]))
    for action in whole:
        action.start()
    before, after = halo.at[0], halo.at[1]
    arrived.wait()

    for d in range(GROUPS):
        total = parts[d, 8:16]
        if d + 1 < GROUPS:
            total += parts[d + 1, 0:8]
        if d > 0:
            total += parts[d - 1, 16:24]
        sums[d + 1] = total
    sums[0] = jnp.zeros((8, BS), f32)
    sums[GROUPS + 1] = jnp.zeros((8, BS), f32)

    entering[0:8] = jnp.zeros((8, BS), f32)
    value = jnp.zeros((1, BS), f32)
    heights = []
    for d in range(GROUPS):
        if d % step == 0:
            for kind in (0, 1):
                chain_copies[kind, d // step].wait()
        own, local = sums[d + 1, 4:5], sums[d + 1, 0:1]
        if d % 2 == 0:
            height = jnp.sum(chain[1, d] * value + jnp.where(eye, local, 0.0), axis=1, keepdims=True)
            value = jnp.sum(chain[0, d] * value + jnp.where(eye, own, 0.0), axis=1, keepdims=True)
            entering[d + 1 : d + 2] = column_to_row(value, eye)
        else:
            height = jnp.sum(chain[1, d] * value, axis=0, keepdims=True) + local
            value = jnp.sum(chain[0, d] * value, axis=0, keepdims=True) + own
            entering[d + 1 : d + 2] = value
        heights.append(column_to_row(height, eye) if d % 2 == 0 else height)
    leaving[GROUPS : GROUPS + 8] = jnp.zeros((8, BS), f32)
    value = None
    for d in reversed(range(GROUPS)):
        if d % step == step - 1:
            chain_copies[2, d // step].wait()
        if d == GROUPS - 1:
            value = heights[d]
        elif d % 2 == 0:
            value = jnp.sum(chain[2, d] * value + jnp.where(eye, heights[d], 0.0), axis=1, keepdims=True)
        else:
            value = jnp.sum(chain[2, d] * value, axis=0, keepdims=True) + heights[d]
        leaving[d : d + 1] = column_to_row(value, eye) if d % 2 == 0 else value

    for action in copies[:3]:
        action.wait()
    for j in range(8):
        offset, block = ((-1, j + 2), (0, j - 2), (1, j - 6))[(j + 2) // 4]
        group = gy + offset
        enter = entering[pl.ds(jnp.maximum(group, 0), 1)]
        leave = leaving[pl.ds(jnp.minimum(group + 1, GROUPS), 1)]
        total = inside[2 * j] * enter + inside[2 * j + 1] * leave
        window[j : j + 1] = column_to_row(jnp.sum(total, axis=1, keepdims=True), eye) + sums[
            group + 1, block : block + 1]
    coarse_out[...] = window[2:6]

    for action in copies[3:]:
        action.wait()
    low_block = gy * 4 - 2
    field[4 : ROWS + 4] = second_own[...]
    left = pl.multiple_of(8 + 8 * jnp.maximum(gx - 1, 0), 8)
    right = pl.multiple_of(8 + 8 * jnp.minimum(gx + 1, 3), 8)
    field[0:4] = shared[pl.ds(left, 8)][4:8]
    field[FEXT - 4 : FEXT] = shared[pl.ds(right, 8)][0:4]

    def interpolate(index, weight):
        block, within = (index >> 7) - low_block, index & 127
        total = jnp.zeros(index.shape, f32)
        for j in range(8):
            source = jnp.broadcast_to(window[j : j + 1], index.shape)
            total = jnp.where(block == j, jnp.take_along_axis(source, within, axis=1), total)
        return weight * total

    for at in range(ROWS // 8):
        rows = pl.ds(8 * at, 8)
        field[pl.ds(8 * at + 4, 8)] += interpolate(indices[rows], weight_rows[rows])
    for top, source in ((0, before), (FEXT - 4, after)):
        index = source[8, 8:16].astype(jnp.int32)
        weight = jnp.concatenate([source[8, 4:8], jnp.zeros((4, BS), f32)], axis=0)
        field[top : top + 4] += interpolate(index, weight)[0:4]

    base = gx * ROWS - 4
    next_field[0:2] = jnp.zeros((2, BS), f32)
    next_field[FEXT - 2 : FEXT] = jnp.zeros((2, BS), f32)
    for action in whole:
        action.wait()

    def third(n, _):
        change = change_row(blocks, 3 * n, turned[n], field, picks_of(columns, n, base))
        rows = pl.ds(n + 4, 1)
        next_field[rows] = field[rows] + first_field[rows] - change
        return 0

    lax.fori_loop(0, ROWS, third, 0, unroll=8)
    for side, source in ((0, before), (1, after)):
        for r in range(2):
            at = side * (ROWS + 2) + 2 + r
            change = change_row(source, 3 * r, source[6 + r], field, halo_picks(halo_columns, side, r, base))
            next_field[at : at + 1] = field[at : at + 1] + first_field[at : at + 1] - change

    def fourth(n, _):
        change = change_row(blocks, 3 * n, turned[n], next_field, picks_of(columns, n, base))
        rows = pl.ds(n + 4, 1)
        field_out[pl.ds(n, 1)] = next_field[rows] + first_field[rows] - change
        return 0

    lax.fori_loop(0, ROWS, fourth, 0, unroll=8)


def per_device(
    rhs, fine_blocks, smoother, columns, aggregates, weights, coarse_lower, coarse_upper, coarse_pivot
):
    rhs, aggregates, weights, columns, smoother = rhs[0], aggregates[0], weights[0], columns.transpose(2, 0, 1), smoother[0]
    fine = fine_blocks.reshape(ROWS * 3, BS, BS)
    dma = pltpu.SemaphoreType.DMA

    maps, mine = pl.pallas_call(
        maps_kernel,
        name="maps",
        out_shape=(shape(3, BS, BS), shape(20, BS, BS)),
        in_specs=[HBM] * 3,
        out_specs=(HBM, HBM),
        scratch_shapes=[pltpu.VMEM((3, BS, BS), f32), pltpu.VMEM((20, BS, BS), f32), dma((3,)), dma((2,))],
        compiler_params=grant(58),
    )(coarse_lower, coarse_upper, coarse_pivot)
    gathered = lax.all_gather(maps, "gy", axis=0)

    to_previous, to_next = pl.pallas_call(
        pack_kernel,
        name="pack",
        out_shape=(shape(9, BS, BS), shape(9, BS, BS)),
        in_specs=[HBM] * 3 + [SMEM] + [HBM] * 2,
        out_specs=(HBM, HBM),
        scratch_shapes=[
            pltpu.VMEM((2, 9, BS, BS), f32), pltpu.VMEM((2, 4, BS, BS), f32), pltpu.VMEM((2, 2, 8, BS), f32),
            pltpu.VMEM((2, 8, BS), jnp.int32), dma((2, 5)), dma((2,)),
        ],
        compiler_params=grant(58),
    )(rhs, weights, aggregates, columns, fine, smoother)
    before = lax.ppermute(to_next, "gx", [(i, i + 1) for i in range(3)])
    after = lax.ppermute(to_previous, "gx", [(i + 1, i) for i in range(3)])

    turned, first = pl.pallas_call(
        first_kernel,
        name="first",
        out_shape=(shape(ROWS, BS, BS), shape(ROWS, BS)),
        in_specs=[HBM] * 2,
        out_specs=(VMEM, VMEM),
        scratch_shapes=[pltpu.VMEM((ROWS, BS, BS), f32), pltpu.VMEM((ROWS, BS), f32), dma((ROWS // CHUNK,)), dma],
        compiler_params=grant(56),
    )(rhs, smoother)

    shared, first_field, second_own = pl.pallas_call(
        presmooth_kernel,
        name="presmooth",
        out_shape=(shape(40, BS), shape(FEXT, BS), shape(ROWS, BS)),
        in_specs=[HBM] * 3 + [SMEM] + [HBM] + [VMEM] * 4,
        out_specs=(VMEM, VMEM, VMEM),
        scratch_shapes=[
            pltpu.VMEM((ROWS * 3, BS, BS), f32), pltpu.VMEM((FEXT, BS), f32), pltpu.VMEM((ROWS, BS), f32),
            pltpu.VMEM((2, ROWS, BS), f32), pltpu.VMEM((ROWS, BS), jnp.int32), pltpu.SMEM((2, 8, BS), f32),
            dma((5,)), dma((ROWS // CHUNK,)),
        ],
        compiler_params=grant(52),
    )(rhs, weights, aggregates, columns, fine, turned, first, before, after)
    previous = lax.ppermute(mine, "gy", [(i, i + 1) for i in range(GROUPS - 1)])
    following = lax.ppermute(mine, "gy", [(i + 1, i) for i in range(GROUPS - 1)])
    for bit in (1, 2):
        shared = shared + lax.ppermute(shared, "gx", [(i, i ^ bit) for i in range(4)])

    spread = pl.pallas_call(
        local_kernel,
        name="local_solutions",
        out_shape=shape(GROUPS, 24, BS),
        in_specs=[VMEM] * 4,
        out_specs=VMEM,
        compiler_params=grant(40),
    )(shared, mine, previous, following)
    parts = lax.all_to_all(spread, "gy", 0, 0)

    field, coarse = pl.pallas_call(
        correct_kernel,
        name="correct",
        out_shape=(shape(ROWS, BS), shape(4, BS)),
        in_specs=[HBM] + [VMEM] * 3 + [HBM] * 2 + [SMEM] + [HBM] * 8,
        out_specs=(VMEM, VMEM),
        scratch_shapes=[
            pltpu.VMEM((GROUPS, 24, BS), f32), pltpu.VMEM((3, GROUPS, BS, BS), f32), pltpu.VMEM((16, BS, BS), f32),
            pltpu.VMEM((ROWS * 3, BS, BS), f32), pltpu.VMEM((ROWS, BS, BS), f32), pltpu.VMEM((2, 9, BS, BS), f32),
            pltpu.VMEM((GROUPS + 2, 8, BS), f32),
            pltpu.VMEM((GROUPS + 8, BS), f32), pltpu.VMEM((GROUPS + 8, BS), f32), pltpu.VMEM((8, BS), f32),
            pltpu.VMEM((FEXT, BS), f32), pltpu.VMEM((FEXT, BS), f32), pltpu.SMEM((2, 8, BS), f32),
            pltpu.VMEM((ROWS, BS), f32), pltpu.VMEM((ROWS, BS), jnp.int32), dma((11,)), dma((3, 4)), dma((4,)),
        ],
        compiler_params=grant(58),
    )(
        parts, shared, first_field, second_own, weights, aggregates, columns, gathered, mine, previous, following,
        fine, turned, before, after,
    )
    return (field[None], coarse)


def solution(mesh):
    return jax.shard_map(
        per_device,
        mesh=mesh,
        in_specs=(
            P("gy", "gx", None),
            P("gy", "gx", None, None, None),
            P("gy", "gx", None, None),
            P("gy", "gx", None),
            P("gy", "gx", None),
            P("gy", "gx", None),
            P("gy", None, None),
            P("gy", None, None),
            P("gy", None, None),
        ),
        out_specs=(P("gy", "gx", None), P("gy", None)),
        check_vma=False,
    )
```

profile of v0, /device:TPU:1, one launch (start us, length us, event | category | flops | bytes accessed | tf_op | source)
XLA Modules:
  0.0 104.3 jit_solution(4689278643231637762)
XLA Ops:
  7.2 0.0 all-gather.3.cloned.1.call-start
  7.2 4.1 %maps.1 = (f32[3,128,128]{2,1,0:T(8,128)}, f32[20,128,128]{2,1,0:T(8,128)}) custom-call(f32[4,128,128]{2,1,0:T(8,128)} %lower.1, f32[4,128,128]{2,1,0:T(8,128)} %upper.1, f32[4,128,128]{2,1,0:T(8,128)} %pivot.1), custom_call_target="tpu_custom_call" | custom-call | tf_op jit(solution)/shard_map/maps/pallas_call | solution.py:449
  11.4 0.0 all-gather.3.cloned.1.call-update
  11.4 4.5 %collective-permute-start.4 = (f32[20,128,128]{2,1,0:T(8,128)}, f32[20,128,128]{2,1,0:T(8,128)S(1)}, u32[]{:S(2)}, u32[]{:S(2)}) collective-permute-start(f32[20,128,128]{2,1,0:T(8,128)} %get-tuple-element.18.mine), channel_id=1, source_target_pairs={{0,1},{1,2},{2,3},{3,4},{4,5},{5,6},{6,7},{7,8},{8,9},{9,10},{10,1... | collective-permute-start | bytes 3932168 | tf_op jit(solution)/shard_map/ppermute | solution.py:498
  15.9 1.9 %collective-permute-start.5 = (f32[20,128,128]{2,1,0:T(8,128)}, f32[20,128,128]{2,1,0:T(8,128)S(1)}, u32[]{:S(2)}, u32[]{:S(2)}) collective-permute-start(f32[20,128,128]{2,1,0:T(8,128)} %get-tuple-element.18.mine), channel_id=1, source_target_pairs={{1,0},{2,1},{3,2},{4,3},{5,4},{6,5},{7,6},{8,7},{9,8},{10,9},{11,1... | collective-permute-start | bytes 3932168 | tf_op jit(solution)/shard_map/ppermute | solution.py:499
  17.8 3.3 %pack.1 = (f32[9,128,128]{2,1,0:T(8,128)}, f32[9,128,128]{2,1,0:T(8,128)}) custom-call(f32[64,128]{1,0:T(8,128)} %bitcast.8, f32[64,128]{1,0:T(8,128)} %bitcast.11, s32[64,128]{1,0:T(8,128)} %bitcast.14, s32[3,1,64]{2,1,0:T(1,128)} %bitcast.17, f32[192,128,128]{2,1,0:T(8,128)} %bitcast.20, f32[64,128,128]{2,1,0:T(8,128)} %bitcast.23), custom_call_target="tpu_custom_call" | custom-call | tf_op jit(solution)/shard_map/pack/pallas_call | solution.py:460
  21.1 0.0 copy-start.5
  21.1 0.0 copy-start.6
  21.1 0.0 copy-start.7
  21.1 0.0 copy-start.12
  21.2 3.4 %collective-permute-start = (f32[9,128,128]{2,1,0:T(8,128)}, f32[9,128,128]{2,1,0:T(8,128)S(1)}, u32[]{:S(2)}, u32[]{:S(2)}) collective-permute-start(f32[9,128,128]{2,1,0:T(8,128)} %get-tuple-element.15), channel_id=1, source_target_pairs={{0,32},{32,64},{64,96},{1,33},{33,65},{65,97},{2,34},{34,66},{66,9... | collective-permute-start | bytes 1769480 | tf_op jit(solution)/shard_map/ppermute | solution.py:472
  24.5 1.3 %collective-permute-start.1 = (f32[9,128,128]{2,1,0:T(8,128)}, f32[9,128,128]{2,1,0:T(8,128)S(1)}, u32[]{:S(2)}, u32[]{:S(2)}) collective-permute-start(f32[9,128,128]{2,1,0:T(8,128)} %get-tuple-element.16), channel_id=1, source_target_pairs={{32,0},{64,32},{96,64},{33,1},{65,33},{97,65},{34,2},{66,34},{98,6... | collective-permute-start | bytes 1769480 | tf_op jit(solution)/shard_map/ppermute | solution.py:473
  25.8 7.1 %first.1 = (f32[64,128,128]{2,1,0:T(8,128)}, f32[64,128]{1,0:T(8,128)}) custom-call(f32[64,128]{1,0:T(8,128)} %bitcast.9, f32[64,128,128]{2,1,0:T(8,128)} %bitcast.24), custom_call_target="tpu_custom_call" | custom-call | tf_op jit(solution)/shard_map/first/pallas_call | solution.py:475
  32.9 3.6 %collective-permute-done.before.before_hbm = f32[9,128,128]{2,1,0:T(8,128)S(1)} collective-permute-done((f32[9,128,128]{2,1,0:T(8,128)}, f32[9,128,128]{2,1,0:T(8,128)S(1)}, u32[]{:S(2)}, u32[]{:S(2)}) %collective-permute-start) | collective-permute-done | bytes 589856 | tf_op jit(solution)/shard_map/ppermute | solution.py:472
  36.6 0.0 copy-start.3
  36.6 4.0 %collective-permute-done.1.after.after_hbm = f32[9,128,128]{2,1,0:T(8,128)S(1)} collective-permute-done((f32[9,128,128]{2,1,0:T(8,128)}, f32[9,128,128]{2,1,0:T(8,128)S(1)}, u32[]{:S(2)}, u32[]{:S(2)}) %collective-permute-start.1) | collective-permute-done | bytes 589856 | tf_op jit(solution)/shard_map/ppermute | solution.py:473
  40.6 0.0 copy-start.4
  40.6 0.0 copy-done.5
  40.6 0.0 copy-done.6
  40.6 0.0 copy-done.7
  40.6 0.0 copy-done.12
  40.6 0.0 copy-start.11
  40.7 0.8 copy-done.11
  41.4 0.0 copy-start
  41.4 11.4 %presmooth.1 = (f32[40,128]{1,0:T(8,128)S(1)}, f32[72,128]{1,0:T(8,128)S(1)}, f32[64,128]{1,0:T(8,128)S(1)}) custom-call(f32[64,128]{1,0:T(8,128)S(1)} %bitcast.10, f32[64,128]{1,0:T(8,128)S(1)} %bitcast.13, s32[64,128]{1,0:T(8,128)S(1)} %bitcast.16, s32[3,1,64]{2,1,0:T(1,128)S(1)} %bitcast.19, f32[192,128,128]{2,1,0:T(8,128)} %bitcast.21, ...), custom_call_target="tpu_custom_call" | custom-call | tf_op jit(solution)/shard_map/presmooth/pallas_call | solution.py:485
  52.8 0.0 copy-done.3
  52.8 0.0 copy-done.4
  52.8 0.0 copy-start.9
  52.9 0.0 copy-start.10
  52.9 1.3 %collective-permute-start.2 = (f32[40,128]{1,0:T(8,128)S(1)}, f32[40,128]{1,0:T(8,128)S(1)}, u32[]{:S(2)}, u32[]{:S(2)}) collective-permute-start(f32[40,128]{1,0:T(8,128)S(1)} %get-tuple-element.17), channel_id=1, source_target_pairs={{0,32},{32,0},{64,96},{96,64},{1,33},{33,1},{65,97},{97,65},{2,34}... | collective-permute-start | bytes 61448 | tf_op jit(solution)/shard_map/ppermute | solution.py:501
  54.2 1.9 %collective-permute-done.2 = f32[40,128]{1,0:T(8,128)S(1)} collective-permute-done((f32[40,128]{1,0:T(8,128)S(1)}, f32[40,128]{1,0:T(8,128)S(1)}, u32[]{:S(2)}, u32[]{:S(2)}) %collective-permute-start.2) | collective-permute-done | bytes 20512 | tf_op jit(solution)/shard_map/ppermute | solution.py:501
  56.1 2.6 %collective-permute-start.3 = (f32[40,128]{1,0:T(8,128)S(1)}, f32[40,128]{1,0:T(8,128)S(1)}, u32[]{:S(2)}, u32[]{:S(2)}) collective-permute-start(f32[40,128]{1,0:T(8,128)S(1)} %add.6), channel_id=1, source_target_pairs={{0,64},{32,96},{64,0},{96,32},{1,65},{33,97},{65,1},{97,33},{2,66}... | collective-permute-start | bytes 61448 | tf_op jit(solution)/shard_map/ppermute | solution.py:501
  58.7 1.6 %collective-permute-done.3 = f32[40,128]{1,0:T(8,128)S(1)} collective-permute-done((f32[40,128]{1,0:T(8,128)S(1)}, f32[40,128]{1,0:T(8,128)S(1)}, u32[]{:S(2)}, u32[]{:S(2)}) %collective-permute-start.3) | collective-permute-done | bytes 20512 | tf_op jit(solution)/shard_map/ppermute | solution.py:501
  60.3 0.0 copy-start.8
  60.3 0.0 collective-permute-done.4.previous
  60.3 0.0 copy-start.1
  60.3 0.0 collective-permute-done.5.following
  60.4 0.0 copy-done
  60.4 0.0 copy-start.2
  60.4 1.3 %local_solutions.1 = f32[32,24,128]{2,1,0:T(8,128)S(1)} custom-call(f32[40,128]{1,0:T(8,128)S(1)} %add.7.shared, f32[20,128,128]{2,1,0:T(8,128)S(1)} %copy-done, f32[20,128,128]{2,1,0:T(8,128)S(1)} %collective-permute-done.4.previous, f32[20,128,128]{2,1,0:T(8,128)S(1)} %collective-permute-done.5.following), custom_call_target="tpu_custom_call" | custom-call | tf_op jit(solution)/shard_map/local_solutions/pallas_call | solution.py:503
  61.7 0.0 copy-done.9
  61.7 0.0 copy-done.10
  61.7 0.0 copy-done.2
  61.8 21.7 %all_to_all.5.parts_hbm = f32[32,24,128]{2,1,0:T(8,128)} all-to-all(f32[32,24,128]{2,1,0:T(8,128)S(1)} %local_solutions.1), channel_id=1, replica_groups=mesh['gx'=4,'gy'=32] {'gy'}, dimensions={0} | all-to-all | bytes 786432 | tf_op jit(solution)/shard_map/all_to_all | solution.py:511
  83.4 0.0 all-gather.3.cloned.1.call-done
  83.5 0.0 copy-done.8
  83.5 0.0 copy-done.1
  83.5 14.0 %correct.1 = (f32[64,128]{1,0:T(8,128)}, f32[4,128]{1,0:T(4,128)}) custom-call(f32[32,24,128]{2,1,0:T(8,128)} %all_to_all.5.parts_hbm, f32[40,128]{1,0:T(8,128)} %copy-done.8, f32[72,128]{1,0:T(8,128)} %copy-done.9, f32[64,128]{1,0:T(8,128)} %copy-done.10, f32[64,128]{1,0:T(8,128)} %bitcast.12, s32[64,128]{1,0:T(8,128)} %bitcast.15, s32[3,1,64]{2,1,0:T(1,128)} %bitcast.18, ...), custom_call_target="tpu_custom_call" | custom-call | tf_op jit(solution)/shard_map/correct/pallas_call | solution.py:513
  (2 shorter events, 0.0 us)
Async XLA Ops:
  7.2 76.3 %all-gather.3.cloned.1.call-start = ((), (), s32[]{:S(2)}) async-start(), calls=%async_computation.1 | async-start | bytes 6488064 | tf_op jit(solution)/shard_map/all_gather | solution.py:458
  11.4 48.9 %collective-permute-start.4 = (f32[20,128,128]{2,1,0:T(8,128)}, f32[20,128,128]{2,1,0:T(8,128)S(1)}, u32[]{:S(2)}, u32[]{:S(2)}) collective-permute-start(f32[20,128,128]{2,1,0:T(8,128)} %get-tuple-element.18.mine), channel_id=1, source_target_pairs={{0,1},{1,2},{2,3},{3,4},{4,5},{5,6},{6,7},{7,8},{8,9},{9,10},{10,1... | collective-permute-start | bytes 3932168 | tf_op jit(solution)/shard_map/ppermute | solution.py:498
  15.9 44.4 %collective-permute-start.5 = (f32[20,128,128]{2,1,0:T(8,128)}, f32[20,128,128]{2,1,0:T(8,128)S(1)}, u32[]{:S(2)}, u32[]{:S(2)}) collective-permute-start(f32[20,128,128]{2,1,0:T(8,128)} %get-tuple-element.18.mine), channel_id=1, source_target_pairs={{1,0},{2,1},{3,2},{4,3},{5,4},{6,5},{7,6},{8,7},{9,8},{10,9},{11,1... | collective-permute-start | bytes 3932168 | tf_op jit(solution)/shard_map/ppermute | solution.py:499
  21.1 19.5 %copy-start.5 = (f32[1,64,128]{2,1,0:T(8,128)S(1)}, f32[1,64,128]{2,1,0:T(8,128)}, u32[]{:S(2)}) copy-start(f32[1,64,128]{2,1,0:T(8,128)} %param.9) | copy-start | bytes 98308
  21.1 19.5 %copy-start.6 = (f32[1,64,128]{2,1,0:T(8,128)S(1)}, f32[1,64,128]{2,1,0:T(8,128)}, u32[]{:S(2)}) copy-start(f32[1,64,128]{2,1,0:T(8,128)} %param.14) | copy-start | bytes 98308
  21.1 19.5 %copy-start.7 = (s32[1,64,128]{2,1,0:T(8,128)S(1)}, s32[1,64,128]{2,1,0:T(8,128)}, u32[]{:S(2)}) copy-start(s32[1,64,128]{2,1,0:T(8,128)} %param.13) | copy-start | bytes 98308
  21.1 19.5 %copy-start.12 = (s32[1,64,3]{1,0,2:T(1,128)S(1)}, s32[1,64,3]{1,0,2:T(1,128)}, u32[]{:S(2)}) copy-start(s32[1,64,3]{1,0,2:T(1,128)} %param.12) | copy-start | bytes 2308
  21.2 15.4 %collective-permute-start = (f32[9,128,128]{2,1,0:T(8,128)}, f32[9,128,128]{2,1,0:T(8,128)S(1)}, u32[]{:S(2)}, u32[]{:S(2)}) collective-permute-start(f32[9,128,128]{2,1,0:T(8,128)} %get-tuple-element.15), channel_id=1, source_target_pairs={{0,32},{32,64},{64,96},{1,33},{33,65},{65,97},{2,34},{34,66},{66,9... | collective-permute-start | bytes 1769480 | tf_op jit(solution)/shard_map/ppermute | solution.py:472
  24.5 16.1 %collective-permute-start.1 = (f32[9,128,128]{2,1,0:T(8,128)}, f32[9,128,128]{2,1,0:T(8,128)S(1)}, u32[]{:S(2)}, u32[]{:S(2)}) collective-permute-start(f32[9,128,128]{2,1,0:T(8,128)} %get-tuple-element.16), channel_id=1, source_target_pairs={{32,0},{64,32},{96,64},{33,1},{65,33},{97,65},{34,2},{66,34},{98,6... | collective-permute-start | bytes 1769480 | tf_op jit(solution)/shard_map/ppermute | solution.py:473
  36.6 16.2 %copy-start.3 = (f32[9,128,128]{2,1,0:T(8,128)}, f32[9,128,128]{2,1,0:T(8,128)S(1)}, u32[]{:S(2)}) copy-start(f32[9,128,128]{2,1,0:T(8,128)S(1)} %collective-permute-done.before.before_hbm) | copy-start | bytes 1769476
  40.6 12.2 %copy-start.4 = (f32[9,128,128]{2,1,0:T(8,128)}, f32[9,128,128]{2,1,0:T(8,128)S(1)}, u32[]{:S(2)}) copy-start(f32[9,128,128]{2,1,0:T(8,128)S(1)} %collective-permute-done.1.after.after_hbm) | copy-start | bytes 1769476
  40.6 0.8 copy-start.11
  41.4 18.9 %copy-start = (f32[20,128,128]{2,1,0:T(8,128)S(1)}, f32[20,128,128]{2,1,0:T(8,128)}, u32[]{:S(2)}) copy-start(f32[20,128,128]{2,1,0:T(8,128)} %get-tuple-element.18.mine) | copy-start | bytes 3932164
  52.8 8.9 %copy-start.9 = (f32[72,128]{1,0:T(8,128)}, f32[72,128]{1,0:T(8,128)S(1)}, u32[]{:S(2)}) copy-start(f32[72,128]{1,0:T(8,128)S(1)} %get-tuple-element.19.first_field) | copy-start | bytes 110596
  52.9 8.9 %copy-start.10 = (f32[64,128]{1,0:T(8,128)}, f32[64,128]{1,0:T(8,128)S(1)}, u32[]{:S(2)}) copy-start(f32[64,128]{1,0:T(8,128)S(1)} %get-tuple-element.20.second_own) | copy-start | bytes 98308
  52.9 3.3 %collective-permute-start.2 = (f32[40,128]{1,0:T(8,128)S(1)}, f32[40,128]{1,0:T(8,128)S(1)}, u32[]{:S(2)}, u32[]{:S(2)}) collective-permute-start(f32[40,128]{1,0:T(8,128)S(1)} %get-tuple-element.17), channel_id=1, source_target_pairs={{0,32},{32,0},{64,96},{96,64},{1,33},{33,1},{65,97},{97,65},{2,34}... | collective-permute-start | bytes 61448 | tf_op jit(solution)/shard_map/ppermute | solution.py:501
  56.1 4.2 %collective-permute-start.3 = (f32[40,128]{1,0:T(8,128)S(1)}, f32[40,128]{1,0:T(8,128)S(1)}, u32[]{:S(2)}, u32[]{:S(2)}) collective-permute-start(f32[40,128]{1,0:T(8,128)S(1)} %add.6), channel_id=1, source_target_pairs={{0,64},{32,96},{64,0},{96,32},{1,65},{33,97},{65,1},{97,33},{2,66}... | collective-permute-start | bytes 61448 | tf_op jit(solution)/shard_map/ppermute | solution.py:501
  60.3 23.1 %copy-start.8 = (f32[40,128]{1,0:T(8,128)}, f32[40,128]{1,0:T(8,128)S(1)}, u32[]{:S(2)}) copy-start(f32[40,128]{1,0:T(8,128)S(1)} %add.7.shared) | copy-start | bytes 61444
  60.3 23.1 %copy-start.1 = (f32[20,128,128]{2,1,0:T(8,128)}, f32[20,128,128]{2,1,0:T(8,128)S(1)}, u32[]{:S(2)}) copy-start(f32[20,128,128]{2,1,0:T(8,128)S(1)} %collective-permute-done.4.previous) | copy-start | bytes 3932164
  60.4 1.4 %copy-start.2 = (f32[20,128,128]{2,1,0:T(8,128)}, f32[20,128,128]{2,1,0:T(8,128)S(1)}, u32[]{:S(2)}) copy-start(f32[20,128,128]{2,1,0:T(8,128)S(1)} %collective-permute-done.5.following) | copy-start | bytes 3932164
Sparse Core Ops, SparseCore 0:
  11.5 56.8 all-gather.2
where the time goes:
time: 105 us; the launch traced here: 104 us
  Pallas kernels  41.2 us (39%)
  blocking collectives  21.7 us (21%)
  starting transfers between devices  15.1 us (14%)
  between operations  14.3 us (14%)
  waiting for transfers between devices  11.2 us (11%)
    all_to_all x1, blocking collectives, per_device(): parts = lax.all_to_all(spread, 'gy', 0, 0)  21.7 us
    pallas_call x1, Pallas kernels, per_device(): pl.pallas_call(correct_kernel, name='correct', out_shape=(shape(ROWS, BS)...  14 us
    pallas_call x1, Pallas kernels, per_device(): pl.pallas_call(presmooth_kernel, name='presmooth', out_shape=(shape(40, B...  11.4 us
    pallas_call x1, Pallas kernels, per_device(): pl.pallas_call(first_kernel, name='first', out_shape=(shape(ROWS, BS, BS)...  7.11 us
    ppermute x1, starting transfers between devices, per_device(): previous = lax.ppermute(mine, 'gy', [(i, i + 1) for i in range(GROUPS - 1)])  4.51 us
    pallas_call x1, Pallas kernels, per_device(): pl.pallas_call(maps_kernel, name='maps', out_shape=(shape(3, BS, BS), sha...  4.14 us
    ppermute x1, waiting for transfers between devices, per_device(): after = lax.ppermute(to_previous, 'gx', [(i + 1, i) for i in range(3)])  4.03 us
    ppermute x2, starting transfers between devices, per_device(): lax.ppermute(shared, 'gx', [(i, i ^ bit) for i in range(4)])  3.94 us
  transfers between devices with their start and end apart: 7, of which 4 were waited for; matrix products, arithmetic and copies ran while one was open for 0% of the time, Pallas kernels for 22%

commit v1 on v0

--- a/solution.py
+++ b/solution.py
@@ -11,6 +11,7 @@
 CHUNK = 8
 LOWER, UPPER, PIVOT, INSIDE = 0, 4, 8, 12
 GROUPS = 32
+TURNED, SMALL, HALO = 768, 1024, 1048
 f32 = jnp.float32
 VMEM = pl.BlockSpec(memory_space=pltpu.VMEM)
 SMEM = pl.BlockSpec(memory_space=pltpu.SMEM)
@@ -88,8 +89,8 @@
 
 
 def pack_kernel(
-    rhs, weights, aggregates, columns, fine, smoother,
-    to_previous, to_next,
+    rhs, weights, aggregates, columns, fine, smoother, mine,
+    to_previous, to_next, mine_out,
     packed, edge, ends, indices, sems, out_sems,
 ):
     eye = identity_mask()
@@ -107,25 +108,25 @@
         near.append(start(weights.at[pl.ds(top, 8)], ends.at[side, 1], side, 2))
         near.append(start(aggregates.at[pl.ds(top, 8)], indices.at[side], side, 3))
     for side in range(2):
-        far.append(start(fine.at[pl.ds(side * (ROWS - 2) * 3, 6)], packed.at[side, pl.ds(0, 6)], side, 4))
+        far.append(start(fine.at[pl.ds(side * (ROWS - 2) * 3 * BS, TURNED)], packed.at[side, pl.ds(0, TURNED)], side, 4))
     for action in near:
         action.wait()
     lane = lax.broadcasted_iota(jnp.int32, (8, BS), 1)
     for side in range(2):
         top = 4 * side
-        packed[side, 6] = edge[side, 2 * side].T
-        packed[side, 7] = edge[side, 2 * side + 1].T
+        packed[side, TURNED : TURNED + BS] = edge[side, 2 * side].T
+        packed[side, TURNED + BS : SMALL] = edge[side, 2 * side + 1].T
         for r in range(4):
-            packed[side, 8, r : r + 1] = times_row(edge[side, r], ends[side, 0, top + r : top + r + 1], eye)
-        packed[side, 8, 4:8] = ends[side, 1, top : top + 4]
-        packed[side, 8, 8:12] = indices[side, top : top + 4].astype(f32)
-        packed[side, 8, 12:16] = jnp.zeros((4, BS), f32)
+            packed[side, SMALL + r : SMALL + r + 1] = times_row(
+                edge[side, r], ends[side, 0, top + r : top + r + 1], eye)
+        packed[side, SMALL + 4 : SMALL + 8] = ends[side, 1, top : top + 4]
+        packed[side, SMALL + 8 : SMALL + 12] = indices[side, top : top + 4].astype(f32)
+        packed[side, SMALL + 12 : SMALL + 16] = jnp.zeros((4, BS), f32)
         picked = jnp.zeros((8, BS), jnp.int32)
         for r in range(2):
             for k in range(3):
                 picked = jnp.where(lane == 3 * r + k, columns[k, 0, side * (ROWS - 2) + r], picked)
-        packed[side, 8, 16:24] = picked.astype(f32)
-        packed[side, 8, 24:BS] = jnp.zeros((BS - 24, BS), f32)
+        packed[side, SMALL + 16 : HALO] = picked.astype(f32)
     for action in far:
         action.wait()
     sent = [
@@ -138,43 +139,25 @@
         action.wait()
 
 
-def first_kernel(rhs, smoother, turned, first, smooth, rhs_rows, sems, rhs_sem):
-    eye = identity_mask()
-    n_chunks = ROWS // CHUNK
-
-    def smooth_copy(c):
-        rows = pl.ds(c * CHUNK, CHUNK)
-        return pltpu.make_async_copy(smoother.at[rows], smooth.at[rows], sems.at[c])
-
-    small = pltpu.make_async_copy(rhs, rhs_rows, rhs_sem)
-    small.start()
-    for c in range(n_chunks):
-        smooth_copy(c).start()
-    small.wait()
-    for c in range(n_chunks):
-        smooth_copy(c).wait()
-
-        def row(r, _):
-            n = c * CHUNK + r
-            block = smooth[n]
-            column = jnp.sum(block * rhs_rows[pl.ds(n, 1)], axis=1, keepdims=True)
-            first[pl.ds(n, 1)] = column_to_row(column, eye)
-            turned[n] = block.T
-            return 0
-
-        lax.fori_loop(0, CHUNK, row, 0, unroll=8)
-
-
-def change_row(blocks, at, turned_block, source, picks):
-    total = blocks[at] * source[pl.ds(picks[0], 1)]
-    total += blocks[at + 1] * source[pl.ds(picks[1], 1)]
-    total += blocks[at + 2] * source[pl.ds(picks[2], 1)]
+def change_row(blocks, turned_block, source, picks):
+    total = blocks[0] * source[pl.ds(picks[0], 1)]
+    total += blocks[1] * source[pl.ds(picks[1], 1)]
+    total += blocks[2] * source[pl.ds(picks[2], 1)]
     column = jnp.sum(total, axis=1, keepdims=True)
     if turned_block is None:
         return column
     return jnp.sum(turned_block * column, axis=0, keepdims=True)
 
 
+def own_blocks(blocks, n):
+    return [blocks[3 * n + k] for k in range(3)]
+
+
+def halo_change(halo, r, source, picks):
+    blocks = [halo[(3 * r + k) * BS : (3 * r + k + 1) * BS] for k in range(3)]
+    return change_row(blocks, halo[TURNED + r * BS : TURNED + (r + 1) * BS], source, picks)
+
+
 def picks_of(columns, n, base):
     return [jnp.clip(columns[k, 0, n] - base, 0, FEXT - 1) for k in range(3)]
 
@@ -184,83 +167,154 @@
         jnp.clip(halo_columns[side, 0, 3 * r + k].astype(jnp.int32) - base, 0, FEXT - 1) for k in range(3)]
 
 
-def presmooth_kernel(
-    rhs, weights, aggregates, columns, fine, turned, first, before, after,
-    shared, first_field, second_own,
-    blocks, second_field, residual, rows, indices, halo_columns, sems, block_sems,
+def scattered(total, value, index, low_block):
+    row8 = lax.broadcasted_iota(jnp.int32, (8, BS), 0)
+    row128 = lax.broadcasted_iota(jnp.int32, (BS, BS), 0)
+    block, within = (index >> 7) - low_block, index & 127
+    value = jnp.where(row8 == block, value, 0.0)
+    high = value.astype(jnp.bfloat16).astype(f32)
+    parts = jnp.concatenate([high, value - high], axis=0).astype(jnp.bfloat16)
+    hot = jnp.where(row128 == within, 1.0, 0.0).astype(jnp.bfloat16)
+    return total + lax.dot_general(parts, hot, (((1,), (1,)), ((), ())), preferred_element_type=f32)
+
+
+def interior_kernel(
+    rhs, weights, aggregates, columns, fine, smoother, packed,
+    turned_out, first_out, second_out, total_out,
+    blocks, smooth, turned, first, second, residual, rows, indices, sems, small_sems, out_sems,
 ):
     gx = lax.axis_index("gx")
-    gy = lax.axis_index("gy")
+    low_block = lax.axis_index("gy") * 4 - 2
     eye = identity_mask()
-    copies = [
-        pltpu.make_async_copy(before.at[8, pl.ds(16, 8)], halo_columns.at[0], sems.at[0]),
-        pltpu.make_async_copy(after.at[8, pl.ds(16, 8)], halo_columns.at[1], sems.at[1]),
-        pltpu.make_async_copy(rhs, rows.at[0], sems.at[2]),
-        pltpu.make_async_copy(weights, rows.at[1], sems.at[3]),
-        pltpu.make_async_copy(aggregates, indices, sems.at[4]),
+    n_chunks = ROWS // CHUNK
+    small = [
+        pltpu.make_async_copy(rhs, rows.at[0], small_sems.at[0]),
+        pltpu.make_async_copy(weights, rows.at[1], small_sems.at[1]),
+        pltpu.make_async_copy(aggregates, indices, small_sems.at[2]),
     ]
-    n_chunks = ROWS // CHUNK
+    for action in small:
+        action.start()
+
+    def fetch(c):
+        part = pl.ds(c * CHUNK, CHUNK)
+        return pltpu.make_async_copy(smoother.at[part], smooth.at[part], sems.at[0, c])
 
     def block_copy(c):
         part = pl.ds(c * CHUNK * 3, CHUNK * 3)
-        return pltpu.make_async_copy(fine.at[part], blocks.at[part], block_sems.at[c])
-
+        return pltpu.make_async_copy(fine.at[part], blocks.at[part], sems.at[1, c])
+
+    def store(c):
+        part = pl.ds(c * CHUNK, CHUNK)
+        return pltpu.make_async_copy(turned.at[part], turned_out.at[part], out_sems.at[c])
+
+    for c in range(n_chunks):
+        fetch(c).start()
     for c in range(n_chunks):
         block_copy(c).start()
-    for action in copies:
-        action.start()
+    for action in small:
+        action.wait()
+
+    def first_row(n, _):
+        block = smooth[n]
+        column = jnp.sum(block * rows[0, pl.ds(n, 1)], axis=1, keepdims=True)
+        first[pl.ds(n, 1)] = column_to_row(column, eye)
+        turned[n] = block.T
+        return 0
+
+    for c in range(n_chunks):
+        fetch(c).wait()
+        lax.fori_loop(c * CHUNK, c * CHUNK + CHUNK, first_row, 0, unroll=8)
+        store(c).start()
+    base = gx * ROWS
+
+    def picks(n):
+        return [jnp.clip(columns[k, 0, n] - base, 0, ROWS - 1) for k in range(3)]
+
+    def second_row(n, _):
+        change = change_row(own_blocks(blocks, n), turned[n], first, picks(n))
+        second[pl.ds(n, 1)] = 2.0 * first[pl.ds(n, 1)] - change
+        return 0
+
+    second[...] = jnp.zeros_like(second)
+    for c in range(n_chunks):
+        block_copy(c).wait()
+        lax.fori_loop(max(c * CHUNK, 2), min(c * CHUNK + CHUNK, ROWS - 2), second_row, 0, unroll=True)
+
+    def residual_row(n, _):
+        column = change_row(own_blocks(blocks, n), None, second, picks(n))
+        residual[pl.ds(n, 1)] = column_to_row(column, eye)
+        return 0
+
+    lax.fori_loop(4, ROWS - 4, residual_row, 0, unroll=8)
+    residual[...] = rows[1] * (rows[0] - residual[...])
+
+    def scatter(n, total):
+        return scattered(total, residual[pl.ds(n, 1)], indices[pl.ds(n, 1)], low_block)
+
+    total_out[...] = lax.fori_loop(4, ROWS - 4, scatter, jnp.zeros((16, BS), f32), unroll=8)
+    first_out[...] = first[...]
+    second_out[...] = second[...]
+    for c in range(n_chunks):
+        store(c).wait()
+
+
+def edges_kernel(
+    rhs, weights, aggregates, columns, fine, turned_hbm, first, second, total_in, before_hbm, after_hbm,
+    shared, first_field, second_own,
+    blocks, turned, halo, field, ends, indices, halo_columns, sems,
+):
+    gx = lax.axis_index("gx")
+    low_block = lax.axis_index("gy") * 4 - 2
+    eye = identity_mask()
+    copies = []
+    for side, source in ((0, before_hbm), (1, after_hbm)):
+        top, near = side * (ROWS - 4), side * (ROWS - 8)
+        for at, (src, dst) in enumerate((
+            (source.at[pl.ds(SMALL + 16, 8)], halo_columns.at[side]),
+            (source, halo.at[side]),
+            (fine.at[pl.ds(3 * top, 12)], blocks.at[side]),
+            (turned_hbm.at[pl.ds(side * (ROWS - 2), 2)], turned.at[side]),
+            (rhs.at[pl.ds(near, 8)], ends.at[side, 0]),
+            (weights.at[pl.ds(near, 8)], ends.at[side, 1]),
+            (aggregates.at[pl.ds(near, 8)], indices.at[side]),
+        )):
+            action = pltpu.make_async_copy(src, dst, sems.at[side, at])
+            action.start()
+            copies.append(action)
     base = gx * ROWS - 4
     first_field[4 : ROWS + 4] = first[...]
-    first_field[0:4] = before[8, 0:4]
-    first_field[FEXT - 4 : FEXT] = after[8, 0:4]
-    second_field[0:2] = jnp.zeros((2, BS), f32)
-    second_field[FEXT - 2 : FEXT] = jnp.zeros((2, BS), f32)
-
-    def second_row(n, _):
-        change = change_row(blocks, 3 * n, turned[n], first_field, picks_of(columns, n, base))
-        second_field[pl.ds(n + 4, 1)] = 2.0 * first_field[pl.ds(n + 4, 1)] - change
-        return 0
-
-    for c in range(n_chunks):
-        block_copy(c).wait()
-        lax.fori_loop(c * CHUNK, c * CHUNK + CHUNK, second_row, 0, unroll=8)
-    copies[0].wait()
-    copies[1].wait()
-    for side, source in ((0, before), (1, after)):
+    field[4 : ROWS + 4] = second[...]
+    field[0:2] = jnp.zeros((2, BS), f32)
+    field[FEXT - 2 : FEXT] = jnp.zeros((2, BS), f32)
+    for action in copies:
+        action.wait()
+    first_field[0:4] = halo[0, SMALL : SMALL + 4]
+    first_field[FEXT - 4 : FEXT] = halo[1, SMALL : SMALL + 4]
+
+    def edge_blocks(side, r):
+        return [blocks[side, 3 * r + k] for k in range(3)]
+
+    for side in range(2):
         for r in range(2):
             at = side * (ROWS + 2) + 2 + r
+            change = halo_change(halo.at[side], r, first_field, halo_picks(halo_columns, side, r, base))
+            field[at : at + 1] = 2.0 * first_field[at : at + 1] - change
+            n = side * (ROWS - 2) + r
             change = change_row(
-                source, 3 * r, source[6 + r], first_field, halo_picks(halo_columns, side, r, base))
-            second_field[at : at + 1] = 2.0 * first_field[at : at + 1] - change
-    second_own[...] = second_field[4 : ROWS + 4]
-
-    def residual_row(n, _):
-        column = change_row(blocks, 3 * n, None, second_field, picks_of(columns, n, base))
-        residual[pl.ds(n, 1)] = column_to_row(column, eye)
-        return 0
-
-    lax.fori_loop(0, ROWS, residual_row, 0, unroll=8)
-    for action in copies[2:]:
-        action.wait()
-    residual[...] = rows[1] * (rows[0] - residual[...])
-    low_block = gy * 4 - 2
-    row8 = lax.broadcasted_iota(jnp.int32, (8, BS), 0)
-    row128 = lax.broadcasted_iota(jnp.int32, (BS, BS), 0)
-
-    def scatter(n, total):
-        index = indices[pl.ds(n, 1)]
-        block, within = (index >> 7) - low_block, index & 127
-        value = jnp.where(row8 == block, residual[pl.ds(n, 1)], 0.0)
-        high = value.astype(jnp.bfloat16).astype(f32)
-        parts = jnp.concatenate([high, value - high], axis=0).astype(jnp.bfloat16)
-        hot = jnp.where(row128 == within, 1.0, 0.0).astype(jnp.bfloat16)
-        return total + lax.dot_general(parts, hot, (((1,), (1,)), ((), ())), preferred_element_type=f32)
-
-    total = lax.fori_loop(0, ROWS, scatter, jnp.zeros((16, BS), f32), unroll=8)
+                edge_blocks(side, 2 * side + r), turned[side, r], first_field, picks_of(columns, n, base))
+            field[n + 4 : n + 5] = 2.0 * first_field[n + 4 : n + 5] - change
+    second_own[...] = field[4 : ROWS + 4]
+    total = total_in[...]
+    for side in range(2):
+        for r in range(4):
+            n, at = side * (ROWS - 4) + r, 4 * side + r
+            column = change_row(edge_blocks(side, r), None, field, picks_of(columns, n, base))
+            value = ends[side, 1, at : at + 1] * (ends[side, 0, at : at + 1] - column_to_row(column, eye))
+            total = scattered(total, value, indices[side, at : at + 1], low_block)
     shared[0:8] = total[0:8] + total[8:16]
     shared[8:40] = jnp.zeros((32, BS), f32)
     shared[pl.ds(pl.multiple_of(8 + 8 * gx, 8), 8)] = jnp.concatenate(
-        [second_field[4:8], second_field[FEXT - 8 : FEXT - 4]], axis=0)
+        [field[4:8], field[FEXT - 8 : FEXT - 4]], axis=0)
 
 
 def local_kernel(shared, mine, previous, following, out):
@@ -305,31 +359,28 @@
     chain_copies = {}
     arrived = pltpu.make_async_copy(parts_hbm, parts, sems.at[4])
     arrived.start()
-    for kind in (0, 1, 2):
-        order = range(GROUPS // step) if kind < 2 else reversed(range(GROUPS // step))
-        for c in order:
-            action = pltpu.make_async_copy(
-                maps.at[pl.ds(c * step, step), kind], chain.at[kind, pl.ds(c * step, step)], chain_sems.at[kind, c])
-            action.start()
-            chain_copies[kind, c] = action
+    n_steps = GROUPS // step
+    for kind, c in [(k, c) for c in range(n_steps) for k in (0, 1)] + [(2, c) for c in reversed(range(n_steps))]:
+        action = pltpu.make_async_copy(
+            maps.at[pl.ds(c * step, step), kind], chain.at[kind, pl.ds(c * step, step)], chain_sems.at[kind, c])
+        action.start()
+        chain_copies[kind, c] = action
     copies = [
         pltpu.make_async_copy(previous.at[pl.ds(INSIDE + 4, 4)], inside.at[pl.ds(0, 4)], sems.at[5]),
         pltpu.make_async_copy(mine.at[pl.ds(INSIDE, 8)], inside.at[pl.ds(4, 8)], sems.at[6]),
         pltpu.make_async_copy(following.at[pl.ds(INSIDE, 4)], inside.at[pl.ds(12, 4)], sems.at[7]),
-        pltpu.make_async_copy(before_hbm.at[8, pl.ds(16, 8)], halo_columns.at[0], sems.at[0]),
-        pltpu.make_async_copy(after_hbm.at[8, pl.ds(16, 8)], halo_columns.at[1], sems.at[1]),
+        pltpu.make_async_copy(before_hbm.at[pl.ds(SMALL + 16, 8)], halo_columns.at[0], sems.at[0]),
+        pltpu.make_async_copy(after_hbm.at[pl.ds(SMALL + 16, 8)], halo_columns.at[1], sems.at[1]),
         pltpu.make_async_copy(weights, weight_rows, sems.at[2]),
         pltpu.make_async_copy(aggregates, indices, sems.at[3]),
         pltpu.make_async_copy(before_hbm, halo.at[0], sems.at[8]),
         pltpu.make_async_copy(after_hbm, halo.at[1], sems.at[9]),
     ]
-    for action in copies:
-        action.start()
     whole = [pltpu.make_async_copy(turned_hbm, turned, sems.at[10])]
     for c in range(4):
         rows = pl.ds(c * (ROWS * 3 // 4), ROWS * 3 // 4)
         whole.append(pltpu.make_async_copy(fine.at[rows], blocks.at[rows], block_sems.at[c]))
-    for action in whole:
+    for action in copies + whole:
         action.start()
     before, after = halo.at[0], halo.at[1]
     arrived.wait()
@@ -407,31 +458,32 @@
         rows = pl.ds(8 * at, 8)
         field[pl.ds(8 * at + 4, 8)] += interpolate(indices[rows], weight_rows[rows])
     for top, source in ((0, before), (FEXT - 4, after)):
-        index = source[8, 8:16].astype(jnp.int32)
-        weight = jnp.concatenate([source[8, 4:8], jnp.zeros((4, BS), f32)], axis=0)
+        index = source[SMALL + 8 : SMALL + 16].astype(jnp.int32)
+        weight = jnp.concatenate([source[SMALL + 4 : SMALL + 8], jnp.zeros((4, BS), f32)], axis=0)
         field[top : top + 4] += interpolate(index, weight)[0:4]
 
     base = gx * ROWS - 4
     next_field[0:2] = jnp.zeros((2, BS), f32)
     next_field[FEXT - 2 : FEXT] = jnp.zeros((2, BS), f32)
-    for action in whole:
-        action.wait()
+    whole[0].wait()
 
     def third(n, _):
-        change = change_row(blocks, 3 * n, turned[n], field, picks_of(columns, n, base))
+        change = change_row(own_blocks(blocks, n), turned[n], field, picks_of(columns, n, base))
         rows = pl.ds(n + 4, 1)
         next_field[rows] = field[rows] + first_field[rows] - change
         return 0
 
-    lax.fori_loop(0, ROWS, third, 0, unroll=8)
+    for c in range(4):
+        whole[1 + c].wait()
+        lax.fori_loop(c * ROWS // 4, (c + 1) * ROWS // 4, third, 0, unroll=8)
     for side, source in ((0, before), (1, after)):
         for r in range(2):
             at = side * (ROWS + 2) + 2 + r
-            change = change_row(source, 3 * r, source[6 + r], field, halo_picks(halo_columns, side, r, base))
+            change = halo_change(source, r, field, halo_picks(halo_columns, side, r, base))
             next_field[at : at + 1] = field[at : at + 1] + first_field[at : at + 1] - change
 
     def fourth(n, _):
-        change = change_row(blocks, 3 * n, turned[n], next_field, picks_of(columns, n, base))
+        change = change_row(own_blocks(blocks, n), turned[n], next_field, picks_of(columns, n, base))
         rows = pl.ds(n + 4, 1)
         field_out[pl.ds(n, 1)] = next_field[rows] + first_field[rows] - change
         return 0
@@ -457,44 +509,50 @@
     )(coarse_lower, coarse_upper, coarse_pivot)
     gathered = lax.all_gather(maps, "gy", axis=0)
 
-    to_previous, to_next = pl.pallas_call(
+    to_previous, to_next, mine = pl.pallas_call(
         pack_kernel,
         name="pack",
-        out_shape=(shape(9, BS, BS), shape(9, BS, BS)),
-        in_specs=[HBM] * 3 + [SMEM] + [HBM] * 2,
-        out_specs=(HBM, HBM),
+        out_shape=(shape(HALO, BS), shape(HALO, BS), shape(20, BS, BS)),
+        in_specs=[HBM] * 3 + [SMEM] + [HBM] * 3,
+        out_specs=(HBM, HBM, HBM),
         scratch_shapes=[
-            pltpu.VMEM((2, 9, BS, BS), f32), pltpu.VMEM((2, 4, BS, BS), f32), pltpu.VMEM((2, 2, 8, BS), f32),
+            pltpu.VMEM((2, HALO, BS), f32), pltpu.VMEM((2, 4, BS, BS), f32), pltpu.VMEM((2, 2, 8, BS), f32),
             pltpu.VMEM((2, 8, BS), jnp.int32), dma((2, 5)), dma((2,)),
         ],
+        input_output_aliases={6: 2},
         compiler_params=grant(58),
-    )(rhs, weights, aggregates, columns, fine, smoother)
+    )(rhs, weights, aggregates, columns, fine_blocks.reshape(ROWS * 3 * BS, BS), smoother, mine)
     before = lax.ppermute(to_next, "gx", [(i, i + 1) for i in range(3)])
     after = lax.ppermute(to_previous, "gx", [(i + 1, i) for i in range(3)])
 
-    turned, first = pl.pallas_call(
-        first_kernel,
-        name="first",
-        out_shape=(shape(ROWS, BS, BS), shape(ROWS, BS)),
-        in_specs=[HBM] * 2,
-        out_specs=(VMEM, VMEM),
-        scratch_shapes=[pltpu.VMEM((ROWS, BS, BS), f32), pltpu.VMEM((ROWS, BS), f32), dma((ROWS // CHUNK,)), dma],
-        compiler_params=grant(56),
-    )(rhs, smoother)
+    turned, first, second, total = pl.pallas_call(
+        interior_kernel,
+        name="interior",
+        out_shape=(shape(ROWS, BS, BS), shape(ROWS, BS), shape(ROWS, BS), shape(16, BS)),
+        in_specs=[HBM] * 3 + [SMEM] + [HBM] * 3,
+        out_specs=(HBM, VMEM, VMEM, VMEM),
+        scratch_shapes=[
+            pltpu.VMEM((ROWS * 3, BS, BS), f32), pltpu.VMEM((ROWS, BS, BS), f32), pltpu.VMEM((ROWS, BS, BS), f32),
+            pltpu.VMEM((ROWS, BS), f32), pltpu.VMEM((ROWS, BS), f32), pltpu.VMEM((ROWS, BS), f32),
+            pltpu.VMEM((2, ROWS, BS), f32), pltpu.VMEM((ROWS, BS), jnp.int32),
+            dma((2, ROWS // CHUNK)), dma((3,)), dma((ROWS // CHUNK,)),
+        ],
+        compiler_params=grant(58),
+    )(rhs, weights, aggregates, columns, fine, smoother, to_next)
 
     shared, first_field, second_own = pl.pallas_call(
-        presmooth_kernel,
-        name="presmooth",
+        edges_kernel,
+        name="edges",
         out_shape=(shape(40, BS), shape(FEXT, BS), shape(ROWS, BS)),
-        in_specs=[HBM] * 3 + [SMEM] + [HBM] + [VMEM] * 4,
+        in_specs=[HBM] * 3 + [SMEM] + [HBM] * 2 + [VMEM] * 3 + [HBM] * 2,
         out_specs=(VMEM, VMEM, VMEM),
         scratch_shapes=[
-            pltpu.VMEM((ROWS * 3, BS, BS), f32), pltpu.VMEM((FEXT, BS), f32), pltpu.VMEM((ROWS, BS), f32),
-            pltpu.VMEM((2, ROWS, BS), f32), pltpu.VMEM((ROWS, BS), jnp.int32), pltpu.SMEM((2, 8, BS), f32),
-            dma((5,)), dma((ROWS // CHUNK,)),
+            pltpu.VMEM((2, 12, BS, BS), f32), pltpu.VMEM((2, 2, BS, BS), f32), pltpu.VMEM((2, HALO, BS), f32),
+            pltpu.VMEM((FEXT, BS), f32), pltpu.VMEM((2, 2, 8, BS), f32), pltpu.VMEM((2, 8, BS), jnp.int32),
+            pltpu.SMEM((2, 8, BS), f32), dma((2, 7)),
         ],
-        compiler_params=grant(52),
-    )(rhs, weights, aggregates, columns, fine, turned, first, before, after)
+        compiler_params=grant(58),
+    )(rhs, weights, aggregates, columns, fine, turned, first, second, total, before, after)
     previous = lax.ppermute(mine, "gy", [(i, i + 1) for i in range(GROUPS - 1)])
     following = lax.ppermute(mine, "gy", [(i + 1, i) for i in range(GROUPS - 1)])
     for bit in (1, 2):
@@ -518,7 +576,7 @@
         out_specs=(VMEM, VMEM),
         scratch_shapes=[
             pltpu.VMEM((GROUPS, 24, BS), f32), pltpu.VMEM((3, GROUPS, BS, BS), f32), pltpu.VMEM((16, BS, BS), f32),
-            pltpu.VMEM((ROWS * 3, BS, BS), f32), pltpu.VMEM((ROWS, BS, BS), f32), pltpu.VMEM((2, 9, BS, BS), f32),
+            pltpu.VMEM((ROWS * 3, BS, BS), f32), pltpu.VMEM((ROWS, BS, BS), f32), pltpu.VMEM((2, HALO, BS), f32),
             pltpu.VMEM((GROUPS + 2, 8, BS), f32),
             pltpu.VMEM((GROUPS + 8, BS), f32), pltpu.VMEM((GROUPS + 8, BS), f32), pltpu.VMEM((8, BS), f32),
             pltpu.VMEM((FEXT, BS), f32), pltpu.VMEM((FEXT, BS), f32), pltpu.SMEM((2, 8, BS), f32),

time: 105 us -> 97.3 us (0.927)
  waiting for transfers between devices: 11.2 us -> 3.07 us
  starting transfers between devices: 15.1 us -> 16.2 us
    ppermute x1, waiting for transfers between devices: 4.03 us -> 0.01 us  [per_device(): after = lax.ppermute(to_previous, 'gx', [(i + 1, i) for i in range(3)])]
    ppermute x1, waiting for transfers between devices: 3.64 us -> 0.01 us  [per_device(): before = lax.ppermute(to_next, 'gx', [(i, i + 1) for i in range(3)])]
    ppermute x2, starting transfers between devices: 3.94 us -> 5.22 us  [per_device(): lax.ppermute(shared, 'gx', [(i, i ^ bit) for i in range(4)])]
  transfers between devices with their start and end apart: 7 -> 7, of which waited for: 4 -> 2; matrix products, arithmetic and copies ran while one was open for 0% -> 1% of each run, Pallas kernels for 22% -> 24%
where the time goes in v1:
time: 97.3 us; the launch traced here: 96.8 us
  Pallas kernels  40.9 us (42%)
  blocking collectives  20.7 us (21%)
  starting transfers between devices  16.2 us (17%)
  between operations  14.2 us (15%)
  waiting for transfers between devices  3.07 us (3%)
  local copies, waits for them, and re-layouts  0.99 us (1%)
    all_to_all x1, blocking collectives, per_device(): parts = lax.all_to_all(spread, 'gy', 0, 0)  20.7 us
    pallas_call x1, Pallas kernels, per_device(): pl.pallas_call(interior_kernel, name='interior', out_shape=(shape(ROWS, B...  15.1 us
    pallas_call x1, Pallas kernels, per_device(): pl.pallas_call(correct_kernel, name='correct', out_shape=(shape(ROWS, BS)...  13.1 us
    ppermute x2, starting transfers between devices, per_device(): lax.ppermute(shared, 'gx', [(i, i ^ bit) for i in range(4)])  5.22 us
    ppermute x1, starting transfers between devices, per_device(): previous = lax.ppermute(mine, 'gy', [(i, i + 1) for i in range(GROUPS - 1)])  4.51 us
    pallas_call x1, Pallas kernels, per_device(): pl.pallas_call(maps_kernel, name='maps', out_shape=(shape(3, BS, BS), sha...  4.13 us
    pallas_call x1, Pallas kernels, per_device(): pl.pallas_call(edges_kernel, name='edges', out_shape=(shape(40, BS), shap...  4.03 us
    ppermute x1, starting transfers between devices, per_device(): before = lax.ppermute(to_next, 'gx', [(i, i + 1) for i in range(3)])  3.23 us
  transfers between devices with their start and end apart: 7, of which 2 were waited for; matrix products, arithmetic and copies ran while one was open for 1% of the time, Pallas kernels for 24%

profile of v1, /device:TPU:1, one launch (start us, length us, event | category | flops | bytes accessed | tf_op | source)
XLA Modules:
  0.0 96.8 jit_solution(16159190738190442532)
XLA Ops:
  7.2 0.0 all-gather.3.cloned.1.call-start
  7.2 4.1 %maps.1 = (f32[3,128,128]{2,1,0:T(8,128)}, f32[20,128,128]{2,1,0:T(8,128)}) custom-call(f32[4,128,128]{2,1,0:T(8,128)} %lower.1, f32[4,128,128]{2,1,0:T(8,128)} %upper.1, f32[4,128,128]{2,1,0:T(8,128)} %pivot.1), custom_call_target="tpu_custom_call" | custom-call | tf_op jit(solution)/shard_map/maps/pallas_call | solution.py:501
  11.3 0.0 all-gather.3.cloned.1.call-update
  11.4 3.2 %pack.1 = (f32[1048,128]{1,0:T(8,128)}, f32[1048,128]{1,0:T(8,128)}, f32[20,128,128]{2,1,0:T(8,128)}) custom-call(f32[64,128]{1,0:T(8,128)} %bitcast.24, f32[64,128]{1,0:T(8,128)} %bitcast.16, s32[64,128]{1,0:T(8,128)} %bitcast.20, s32[3,1,64]{2,1,0:T(1,128)} %bitcast.27, f32[24576,128]{1,0:T(8,128)} %bitcast.9, ...), custom_call_target="tpu_custom_call", output_to_operand_aliasing={{2}: (6, {})} | custom-call | tf_op jit(solution)/shard_map/pack/pallas_call | solution.py:512
  14.5 4.5 %collective-permute-start.4 = (f32[20,128,128]{2,1,0:T(8,128)}, f32[20,128,128]{2,1,0:T(8,128)S(1)}, u32[]{:S(2)}, u32[]{:S(2)}) collective-permute-start(f32[20,128,128]{2,1,0:T(8,128)} %get-tuple-element.24.mine), channel_id=1, source_target_pairs={{0,1},{1,2},{2,3},{3,4},{4,5},{5,6},{6,7},{7,8},{8,9},{9,10},{10,1... | collective-permute-start | bytes 3932168 | tf_op jit(solution)/shard_map/ppermute | solution.py:556
  19.1 1.9 %collective-permute-start.5 = (f32[20,128,128]{2,1,0:T(8,128)}, f32[20,128,128]{2,1,0:T(8,128)S(1)}, u32[]{:S(2)}, u32[]{:S(2)}) collective-permute-start(f32[20,128,128]{2,1,0:T(8,128)} %get-tuple-element.24.mine), channel_id=1, source_target_pairs={{1,0},{2,1},{3,2},{4,3},{5,4},{6,5},{7,6},{8,7},{9,8},{10,9},{11,1... | collective-permute-start | bytes 3932168 | tf_op jit(solution)/shard_map/ppermute | solution.py:557
  21.0 3.2 %collective-permute-start = (f32[1048,128]{1,0:T(8,128)}, f32[1048,128]{1,0:T(8,128)S(1)}, u32[]{:S(2)}, u32[]{:S(2)}) collective-permute-start(f32[1048,128]{1,0:T(8,128)} %get-tuple-element.17.packed), channel_id=1, source_target_pairs={{0,32},{32,64},{64,96},{1,33},{33,65},{65,97},{2,34},{34,66},{66,9... | collective-permute-start | bytes 1609736 | tf_op jit(solution)/shard_map/ppermute | solution.py:525
  24.2 1.3 %collective-permute-start.1 = (f32[1048,128]{1,0:T(8,128)}, f32[1048,128]{1,0:T(8,128)S(1)}, u32[]{:S(2)}, u32[]{:S(2)}) collective-permute-start(f32[1048,128]{1,0:T(8,128)} %get-tuple-element.22), channel_id=1, source_target_pairs={{32,0},{64,32},{96,64},{33,1},{65,33},{97,65},{34,2},{66,34},{98,6... | collective-permute-start | bytes 1609736 | tf_op jit(solution)/shard_map/ppermute | solution.py:526
  25.5 15.1 %interior.1 = (f32[64,128,128]{2,1,0:T(8,128)}, f32[64,128]{1,0:T(8,128)}, f32[64,128]{1,0:T(8,128)}, f32[16,128]{1,0:T(8,128)}) custom-call(f32[64,128]{1,0:T(8,128)} %bitcast.25, f32[64,128]{1,0:T(8,128)} %bitcast.17, s32[64,128]{1,0:T(8,128)} %bitcast.21, s32[3,1,64]{2,1,0:T(1,128)} %bitcast.28, f32[192,128,128]{2,1,0:T(8,128)} %bitcast.10, ...), custom_call_target="tpu_custom_call" | custom-call | tf_op jit(solution)/shard_map/interior/pallas_call | solution.py:528
  40.6 0.0 collective-permute-done.before_hbm
  40.6 0.0 copy-start.4
  40.7 0.0 collective-permute-done.1.after_hbm
  40.7 0.0 copy-start.5
  40.7 0.8 copy-done.4
  41.5 0.2 copy-done.5
  41.6 0.0 copy-start
  41.6 4.0 %edges.1 = (f32[40,128]{1,0:T(8,128)}, f32[72,128]{1,0:T(8,128)}, f32[64,128]{1,0:T(8,128)}) custom-call(f32[64,128]{1,0:T(8,128)} %bitcast.26, f32[64,128]{1,0:T(8,128)} %bitcast.18, s32[64,128]{1,0:T(8,128)} %bitcast.22, s32[3,1,64]{2,1,0:T(1,128)} %bitcast.29, f32[192,128,128]{2,1,0:T(8,128)} %bitcast.11, f32[64,128,128]{2,1,0:T(8,128)} %get-tuple-element.18.turned_hbm, ...), custom_call_target="tpu_custom_call" | custom-call | tf_op jit(solution)/shard_map/edges/pallas_call | solution.py:543
  45.7 2.2 %collective-permute-start.2 = (f32[40,128]{1,0:T(8,128)}, f32[40,128]{1,0:T(8,128)S(1)}, u32[]{:S(2)}, u32[]{:S(2)}) collective-permute-start(f32[40,128]{1,0:T(8,128)} %get-tuple-element.23), channel_id=1, source_target_pairs={{0,32},{32,0},{64,96},{96,64},{1,33},{33,1},{65,97},{97,65},{2,34}... | collective-permute-start | bytes 61448 | tf_op jit(solution)/shard_map/ppermute | solution.py:559
  47.9 1.4 %collective-permute-done.2 = f32[40,128]{1,0:T(8,128)S(1)} collective-permute-done((f32[40,128]{1,0:T(8,128)}, f32[40,128]{1,0:T(8,128)S(1)}, u32[]{:S(2)}, u32[]{:S(2)}) %collective-permute-start.2) | collective-permute-done | bytes 20512 | tf_op jit(solution)/shard_map/ppermute | solution.py:559
  49.2 0.7 add.6
  50.0 3.0 %collective-permute-start.3 = (f32[40,128]{1,0:T(8,128)S(1)}, f32[40,128]{1,0:T(8,128)S(1)}, u32[]{:S(2)}, u32[]{:S(2)}) collective-permute-start(f32[40,128]{1,0:T(8,128)S(1)} %add.6), channel_id=1, source_target_pairs={{0,64},{32,96},{64,0},{96,32},{1,65},{33,97},{65,1},{97,33},{2,66}... | collective-permute-start | bytes 61448 | tf_op jit(solution)/shard_map/ppermute | solution.py:559
  53.0 1.7 %collective-permute-done.3 = f32[40,128]{1,0:T(8,128)S(1)} collective-permute-done((f32[40,128]{1,0:T(8,128)S(1)}, f32[40,128]{1,0:T(8,128)S(1)}, u32[]{:S(2)}, u32[]{:S(2)}) %collective-permute-start.3) | collective-permute-done | bytes 20512 | tf_op jit(solution)/shard_map/ppermute | solution.py:559
  54.7 0.0 copy-start.3
  54.7 0.0 collective-permute-done.4.previous
  54.7 0.0 copy-start.1
  54.7 0.0 collective-permute-done.5.following
  54.7 0.0 copy-done
  54.7 0.0 copy-start.2
  54.7 1.3 %local_solutions.1 = f32[32,24,128]{2,1,0:T(8,128)S(1)} custom-call(f32[40,128]{1,0:T(8,128)S(1)} %add.7.shared, f32[20,128,128]{2,1,0:T(8,128)S(1)} %copy-done, f32[20,128,128]{2,1,0:T(8,128)S(1)} %collective-permute-done.4.previous, f32[20,128,128]{2,1,0:T(8,128)S(1)} %collective-permute-done.5.following), custom_call_target="tpu_custom_call" | custom-call | tf_op jit(solution)/shard_map/local_solutions/pallas_call | solution.py:561
  56.1 0.0 copy-done.2
  56.1 20.7 %all_to_all.5.parts_hbm = f32[32,24,128]{2,1,0:T(8,128)} all-to-all(f32[32,24,128]{2,1,0:T(8,128)S(1)} %local_solutions.1), channel_id=1, replica_groups=mesh['gx'=4,'gy'=32] {'gy'}, dimensions={0} | all-to-all | bytes 786432 | tf_op jit(solution)/shard_map/all_to_all | solution.py:569
  76.8 0.0 all-gather.3.cloned.1.call-done
  76.8 0.0 copy-done.3
  76.8 0.0 copy-done.1
  76.9 13.1 %correct.1 = (f32[64,128]{1,0:T(8,128)}, f32[4,128]{1,0:T(4,128)}) custom-call(f32[32,24,128]{2,1,0:T(8,128)} %all_to_all.5.parts_hbm, f32[40,128]{1,0:T(8,128)} %copy-done.3, f32[72,128]{1,0:T(8,128)} %get-tuple-element.25.first_field, f32[64,128]{1,0:T(8,128)} %get-tuple-element.26.second_own, f32[64,128]{1,0:T(8,128)} %bitcast.19, s32[64,128]{1,0:T(8,128)} %bitcast.23, ...), custom_call_target="tpu_custom_call" | custom-call | tf_op jit(solution)/shard_map/correct/pallas_call | solution.py:571
  (1 shorter events, 0.0 us)
Async XLA Ops:
  7.2 69.7 %all-gather.3.cloned.1.call-start = ((), (), s32[]{:S(2)}) async-start(), calls=%async_computation.1 | async-start | bytes 6488064 | tf_op jit(solution)/shard_map/all_gather | solution.py:510
  14.5 40.2 %collective-permute-start.4 = (f32[20,128,128]{2,1,0:T(8,128)}, f32[20,128,128]{2,1,0:T(8,128)S(1)}, u32[]{:S(2)}, u32[]{:S(2)}) collective-permute-start(f32[20,128,128]{2,1,0:T(8,128)} %get-tuple-element.24.mine), channel_id=1, source_target_pairs={{0,1},{1,2},{2,3},{3,4},{4,5},{5,6},{6,7},{7,8},{8,9},{9,10},{10,1... | collective-permute-start | bytes 3932168 | tf_op jit(solution)/shard_map/ppermute | solution.py:556
  19.1 35.7 %collective-permute-start.5 = (f32[20,128,128]{2,1,0:T(8,128)}, f32[20,128,128]{2,1,0:T(8,128)S(1)}, u32[]{:S(2)}, u32[]{:S(2)}) collective-permute-start(f32[20,128,128]{2,1,0:T(8,128)} %get-tuple-element.24.mine), channel_id=1, source_target_pairs={{1,0},{2,1},{3,2},{4,3},{5,4},{6,5},{7,6},{8,7},{9,8},{10,9},{11,1... | collective-permute-start | bytes 3932168 | tf_op jit(solution)/shard_map/ppermute | solution.py:557
  21.0 19.6 %collective-permute-start = (f32[1048,128]{1,0:T(8,128)}, f32[1048,128]{1,0:T(8,128)S(1)}, u32[]{:S(2)}, u32[]{:S(2)}) collective-permute-start(f32[1048,128]{1,0:T(8,128)} %get-tuple-element.17.packed), channel_id=1, source_target_pairs={{0,32},{32,64},{64,96},{1,33},{33,65},{65,97},{2,34},{34,66},{66,9... | collective-permute-start | bytes 1609736 | tf_op jit(solution)/shard_map/ppermute | solution.py:525
  24.2 16.4 %collective-permute-start.1 = (f32[1048,128]{1,0:T(8,128)}, f32[1048,128]{1,0:T(8,128)S(1)}, u32[]{:S(2)}, u32[]{:S(2)}) collective-permute-start(f32[1048,128]{1,0:T(8,128)} %get-tuple-element.22), channel_id=1, source_target_pairs={{32,0},{64,32},{96,64},{33,1},{65,33},{97,65},{34,2},{66,34},{98,6... | collective-permute-start | bytes 1609736 | tf_op jit(solution)/shard_map/ppermute | solution.py:526
  40.6 0.8 copy-start.4
  40.7 1.0 %copy-start.5 = (f32[1048,128]{1,0:T(8,128)}, f32[1048,128]{1,0:T(8,128)S(1)}, u32[]{:S(2)}) copy-start(f32[1048,128]{1,0:T(8,128)S(1)} %collective-permute-done.1.after_hbm) | copy-start | bytes 1609732
  41.6 13.1 %copy-start = (f32[20,128,128]{2,1,0:T(8,128)S(1)}, f32[20,128,128]{2,1,0:T(8,128)}, u32[]{:S(2)}) copy-start(f32[20,128,128]{2,1,0:T(8,128)} %get-tuple-element.24.mine) | copy-start | bytes 3932164
  45.7 3.6 %collective-permute-start.2 = (f32[40,128]{1,0:T(8,128)}, f32[40,128]{1,0:T(8,128)S(1)}, u32[]{:S(2)}, u32[]{:S(2)}) collective-permute-start(f32[40,128]{1,0:T(8,128)} %get-tuple-element.23), channel_id=1, source_target_pairs={{0,32},{32,0},{64,96},{96,64},{1,33},{33,1},{65,97},{97,65},{2,34}... | collective-permute-start | bytes 61448 | tf_op jit(solution)/shard_map/ppermute | solution.py:559
  50.0 4.7 %collective-permute-start.3 = (f32[40,128]{1,0:T(8,128)S(1)}, f32[40,128]{1,0:T(8,128)S(1)}, u32[]{:S(2)}, u32[]{:S(2)}) collective-permute-start(f32[40,128]{1,0:T(8,128)S(1)} %add.6), channel_id=1, source_target_pairs={{0,64},{32,96},{64,0},{96,32},{1,65},{33,97},{65,1},{97,33},{2,66}... | collective-permute-start | bytes 61448 | tf_op jit(solution)/shard_map/ppermute | solution.py:559
  54.7 22.2 %copy-start.3 = (f32[40,128]{1,0:T(8,128)}, f32[40,128]{1,0:T(8,128)S(1)}, u32[]{:S(2)}) copy-start(f32[40,128]{1,0:T(8,128)S(1)} %add.7.shared) | copy-start | bytes 61444
  54.7 22.1 %copy-start.1 = (f32[20,128,128]{2,1,0:T(8,128)}, f32[20,128,128]{2,1,0:T(8,128)S(1)}, u32[]{:S(2)}) copy-start(f32[20,128,128]{2,1,0:T(8,128)S(1)} %collective-permute-done.4.previous) | copy-start | bytes 3932164
  54.7 1.4 %copy-start.2 = (f32[20,128,128]{2,1,0:T(8,128)}, f32[20,128,128]{2,1,0:T(8,128)S(1)}, u32[]{:S(2)}) copy-start(f32[20,128,128]{2,1,0:T(8,128)S(1)} %collective-permute-done.5.following) | copy-start | bytes 3932164
Sparse Core Ops, SparseCore 0:
  11.5 64.3 all-gather.2

commit v2 on v1

--- a/solution.py
+++ b/solution.py
@@ -9,7 +9,7 @@
 ROWS = 64
 FEXT = ROWS + 8
 CHUNK = 8
-LOWER, UPPER, PIVOT, INSIDE = 0, 4, 8, 12
+LOWER, UPPER, PIVOT, MINE, FOR_PREVIOUS, FOR_NEXT = 3, 7, 10, 18, 14, 12
 GROUPS = 32
 TURNED, SMALL, HALO = 768, 1024, 1048
 f32 = jnp.float32
@@ -55,45 +55,26 @@
     )
 
 
-def maps_kernel(lower, upper, pivot, maps_out, mine_out, maps, mine, sems, out_sems):
-    coarse = [
-        pltpu.make_async_copy(source, mine.at[pl.ds(4 * at, 4)], sems.at[at])
-        for at, source in enumerate((lower, upper, pivot))
-    ]
+def inside_at(j):
+    return 2 * j if j < 2 else 10 + 2 * j
+
+
+def prepare_kernel(
+    lower, upper, pivot, rhs, weights, aggregates, columns, fine, smoother,
+    maps_out, mine_out, for_previous, for_next, to_previous, to_next,
+    maps, mine, spare, packed, edge, ends, indices, coarse_sems, sems, out_sems,
+):
+    eye = identity_mask()
+    parts = (
+        (lower.at[pl.ds(0, 1)], spare.at[pl.ds(0, 1)]),
+        (lower.at[pl.ds(1, 3)], mine.at[pl.ds(LOWER + 1, 3)]),
+        (pivot, mine.at[pl.ds(PIVOT, 4)]),
+        (upper.at[pl.ds(3, 1)], spare.at[pl.ds(1, 1)]),
+        (upper.at[pl.ds(0, 3)], mine.at[pl.ds(UPPER, 3)]),
+    )
+    coarse = [pltpu.make_async_copy(src, dst, coarse_sems.at[at]) for at, (src, dst) in enumerate(parts)]
     for action in coarse:
         action.start()
-    coarse[0].wait()
-    forward = [-mine[LOWER]]
-    for j in range(1, 4):
-        forward.append(-product(mine[LOWER + j], forward[-1]))
-    for action in coarse[1:]:
-        action.wait()
-    both = product(mine[PIVOT + 3], jnp.concatenate([forward[3], -mine[UPPER + 3]], axis=1))
-    for j in (3, 2, 1, 0):
-        if j < 3:
-            both = product(mine[UPPER + j], both)
-            both = product(mine[PIVOT + j], jnp.concatenate([forward[j] - both[:, :BS], -both[:, BS:]], axis=1))
-        mine[INSIDE + 2 * j] = both[:, :BS]
-        mine[INSIDE + 2 * j + 1] = both[:, BS:]
-    odd = lax.axis_index("gy") % 2 == 1
-    for at, value in enumerate((forward[3], both[:, :BS], both[:, BS:])):
-        maps[at] = jnp.where(odd, value.T, value)
-    sent = [
-        pltpu.make_async_copy(maps, maps_out, out_sems.at[0]),
-        pltpu.make_async_copy(mine, mine_out, out_sems.at[1]),
-    ]
-    for action in sent:
-        action.start()
-    for action in sent:
-        action.wait()
-
-
-def pack_kernel(
-    rhs, weights, aggregates, columns, fine, smoother, mine,
-    to_previous, to_next, mine_out,
-    packed, edge, ends, indices, sems, out_sems,
-):
-    eye = identity_mask()
 
     def start(source, target, *at):
         action = pltpu.make_async_copy(source, target, sems.at[at])
@@ -109,7 +90,7 @@
         near.append(start(aggregates.at[pl.ds(top, 8)], indices.at[side], side, 3))
     for side in range(2):
         far.append(start(fine.at[pl.ds(side * (ROWS - 2) * 3 * BS, TURNED)], packed.at[side, pl.ds(0, TURNED)], side, 4))
-    for action in near:
+    for action in coarse + near:
         action.wait()
     lane = lax.broadcasted_iota(jnp.int32, (8, BS), 1)
     for side in range(2):
@@ -127,11 +108,28 @@
             for k in range(3):
                 picked = jnp.where(lane == 3 * r + k, columns[k, 0, side * (ROWS - 2) + r], picked)
         packed[side, SMALL + 16 : HALO] = picked.astype(f32)
+    forward = [-spare[0]]
+    for j in range(1, 4):
+        forward.append(-product(mine[LOWER + j], forward[-1]))
+    both = product(mine[PIVOT + 3], jnp.concatenate([forward[3], -spare[1]], axis=1))
+    for j in (3, 2, 1, 0):
+        if j < 3:
+            both = product(mine[UPPER + j], both)
+            both = product(mine[PIVOT + j], jnp.concatenate([forward[j] - both[:, :BS], -both[:, BS:]], axis=1))
+        mine[inside_at(j)] = both[:, :BS]
+        mine[inside_at(j) + 1] = both[:, BS:]
+    odd = lax.axis_index("gy") % 2 == 1
+    for at, value in enumerate((forward[3], both[:, :BS], both[:, BS:])):
+        maps[at] = jnp.where(odd, value.T, value)
     for action in far:
         action.wait()
     sent = [
-        pltpu.make_async_copy(packed.at[side], target, out_sems.at[side])
-        for side, target in enumerate((to_previous, to_next))
+        pltpu.make_async_copy(packed.at[0], to_previous, out_sems.at[4]),
+        pltpu.make_async_copy(packed.at[1], to_next, out_sems.at[5]),
+        pltpu.make_async_copy(maps, maps_out, out_sems.at[0]),
+        pltpu.make_async_copy(mine, mine_out, out_sems.at[1]),
+        pltpu.make_async_copy(mine.at[pl.ds(0, FOR_PREVIOUS)], for_previous, out_sems.at[2]),
+        pltpu.make_async_copy(mine.at[pl.ds(MINE - FOR_NEXT, FOR_NEXT)], for_next, out_sems.at[3]),
     ]
     for action in sent:
         action.start()
@@ -259,19 +257,19 @@
 
 
 def edges_kernel(
-    rhs, weights, aggregates, columns, fine, turned_hbm, first, second, total_in, before_hbm, after_hbm,
+    rhs, weights, aggregates, columns, fine, turned_hbm, first, second, total_in, before, after,
     shared, first_field, second_own,
-    blocks, turned, halo, field, ends, indices, halo_columns, sems,
+    blocks, turned, field, ends, indices, halo_columns, sems,
 ):
     gx = lax.axis_index("gx")
     low_block = lax.axis_index("gy") * 4 - 2
     eye = identity_mask()
     copies = []
-    for side, source in ((0, before_hbm), (1, after_hbm)):
+    halo = (before, after)
+    for side, source in enumerate(halo):
         top, near = side * (ROWS - 4), side * (ROWS - 8)
         for at, (src, dst) in enumerate((
             (source.at[pl.ds(SMALL + 16, 8)], halo_columns.at[side]),
-            (source, halo.at[side]),
             (fine.at[pl.ds(3 * top, 12)], blocks.at[side]),
             (turned_hbm.at[pl.ds(side * (ROWS - 2), 2)], turned.at[side]),
             (rhs.at[pl.ds(near, 8)], ends.at[side, 0]),
@@ -288,8 +286,8 @@
     field[FEXT - 2 : FEXT] = jnp.zeros((2, BS), f32)
     for action in copies:
         action.wait()
-    first_field[0:4] = halo[0, SMALL : SMALL + 4]
-    first_field[FEXT - 4 : FEXT] = halo[1, SMALL : SMALL + 4]
+    first_field[0:4] = before[SMALL : SMALL + 4]
+    first_field[FEXT - 4 : FEXT] = after[SMALL : SMALL + 4]
 
     def edge_blocks(side, r):
         return [blocks[side, 3 * r + k] for k in range(3)]
@@ -297,7 +295,7 @@
     for side in range(2):
         for r in range(2):
             at = side * (ROWS + 2) + 2 + r
-            change = halo_change(halo.at[side], r, first_field, halo_picks(halo_columns, side, r, base))
+            change = halo_change(halo[side], r, first_field, halo_picks(halo_columns, side, r, base))
             field[at : at + 1] = 2.0 * first_field[at : at + 1] - change
             n = side * (ROWS - 2) + r
             change = change_row(
@@ -322,21 +320,25 @@
     zero = jnp.zeros((1, BS), f32)
     own = [shared[j : j + 1] for j in range(8)]
     groups = (
-        (previous, [zero, zero, own[0], own[1]]),
-        (mine, own[2:6]),
-        (following, [own[6], own[7], zero, zero]),
+        (previous, MINE - FOR_NEXT, [zero, zero, own[0], own[1]]),
+        (mine, 0, own[2:6]),
+        (following, 0, [own[6], own[7], zero, zero]),
     )
-    inner = [[right[0]] for _, right in groups]
+    inner = [[right[0]] for _, _, right in groups]
     for j in range(1, 4):
-        for (source, right), found in zip(groups, inner):
-            found.append(right[j] - times_row(source[LOWER + j], found[-1], eye))
+        for at, ((source, start, right), found) in enumerate(zip(groups, inner)):
+            if at == 0 and j < 3:
+                found.append(right[j])
+            else:
+                found.append(right[j] - times_row(source[LOWER + j - start], found[-1], eye))
     solved = [[None] * 4 for _ in groups]
     for j in (3, 2, 1, 0):
         held = []
-        for (source, _), found, x in zip(groups, inner, solved):
-            held.append(found[j] if j == 3 else found[j] - times_row(source[UPPER + j], x[j + 1], eye))
-        for (source, _), value, x in zip(groups, held, solved):
-            x[j] = times_row(source[PIVOT + j], value, eye)
+        for (source, start, _), found, x in zip(groups, inner, solved):
+            held.append(
+                found[j] if j == 3 else found[j] - times_row(source[UPPER + j - start], x[j + 1], eye))
+        for (source, start, _), value, x in zip(groups, held, solved):
+            x[j] = times_row(source[PIVOT + j - start], value, eye)
     tiles = []
     for found, x in zip(inner, solved):
         tiles += x + [found[3], zero, zero, zero]
@@ -366,9 +368,10 @@
         action.start()
         chain_copies[kind, c] = action
     copies = [
-        pltpu.make_async_copy(previous.at[pl.ds(INSIDE + 4, 4)], inside.at[pl.ds(0, 4)], sems.at[5]),
-        pltpu.make_async_copy(mine.at[pl.ds(INSIDE, 8)], inside.at[pl.ds(4, 8)], sems.at[6]),
-        pltpu.make_async_copy(following.at[pl.ds(INSIDE, 4)], inside.at[pl.ds(12, 4)], sems.at[7]),
+        pltpu.make_async_copy(previous.at[pl.ds(FOR_NEXT - 4, 4)], inside.at[pl.ds(0, 4)], sems.at[5]),
+        pltpu.make_async_copy(mine.at[pl.ds(0, 4)], inside.at[pl.ds(4, 4)], sems.at[6]),
+        pltpu.make_async_copy(mine.at[pl.ds(MINE - 4, 4)], inside.at[pl.ds(8, 4)], sems.at[11]),
+        pltpu.make_async_copy(following.at[pl.ds(0, 4)], inside.at[pl.ds(12, 4)], sems.at[7]),
         pltpu.make_async_copy(before_hbm.at[pl.ds(SMALL + 16, 8)], halo_columns.at[0], sems.at[0]),
         pltpu.make_async_copy(after_hbm.at[pl.ds(SMALL + 16, 8)], halo_columns.at[1], sems.at[1]),
         pltpu.make_async_copy(weights, weight_rows, sems.at[2]),
@@ -425,7 +428,7 @@
             value = jnp.sum(chain[2, d] * value, axis=0, keepdims=True) + heights[d]
         leaving[d : d + 1] = column_to_row(value, eye) if d % 2 == 0 else value
 
-    for action in copies[:3]:
+    for action in copies[:4]:
         action.wait()
     for j in range(8):
         offset, block = ((-1, j + 2), (0, j - 2), (1, j - 6))[(j + 2) // 4]
@@ -437,7 +440,7 @@
             group + 1, block : block + 1]
     coarse_out[...] = window[2:6]
 
-    for action in copies[3:]:
+    for action in copies[4:]:
         action.wait()
     low_block = gy * 4 - 2
     field[4 : ROWS + 4] = second_own[...]
@@ -498,30 +501,26 @@
     fine = fine_blocks.reshape(ROWS * 3, BS, BS)
     dma = pltpu.SemaphoreType.DMA
 
-    maps, mine = pl.pallas_call(
-        maps_kernel,
-        name="maps",
-        out_shape=(shape(3, BS, BS), shape(20, BS, BS)),
-        in_specs=[HBM] * 3,
-        out_specs=(HBM, HBM),
-        scratch_shapes=[pltpu.VMEM((3, BS, BS), f32), pltpu.VMEM((20, BS, BS), f32), dma((3,)), dma((2,))],
+    maps, mine, for_previous, for_next, to_previous, to_next = pl.pallas_call(
+        prepare_kernel,
+        name="prepare",
+        out_shape=(
+            shape(3, BS, BS), shape(MINE, BS, BS), shape(FOR_PREVIOUS, BS, BS), shape(FOR_NEXT, BS, BS),
+            shape(HALO, BS), shape(HALO, BS)),
+        in_specs=[HBM] * 6 + [SMEM] + [HBM] * 2,
+        out_specs=(HBM,) * 6,
+        scratch_shapes=[
+            pltpu.VMEM((3, BS, BS), f32), pltpu.VMEM((MINE, BS, BS), f32), pltpu.VMEM((2, BS, BS), f32),
+            pltpu.VMEM((2, HALO, BS), f32), pltpu.VMEM((2, 4, BS, BS), f32), pltpu.VMEM((2, 2, 8, BS), f32),
+            pltpu.VMEM((2, 8, BS), jnp.int32), dma((5,)), dma((2, 5)), dma((6,)),
+        ],
         compiler_params=grant(58),
-    )(coarse_lower, coarse_upper, coarse_pivot)
+    )(
+        coarse_lower, coarse_upper, coarse_pivot, rhs, weights, aggregates, columns,
+        fine_blocks.reshape(ROWS * 3 * BS, BS), smoother,
+    )
     gathered = lax.all_gather(maps, "gy", axis=0)
 
-    to_previous, to_next, mine = pl.pallas_call(
-        pack_kernel,
-        name="pack",
-        out_shape=(shape(HALO, BS), shape(HALO, BS), shape(20, BS, BS)),
-        in_specs=[HBM] * 3 + [SMEM] + [HBM] * 3,
-        out_specs=(HBM, HBM, HBM),
-        scratch_shapes=[
-            pltpu.VMEM((2, HALO, BS), f32), pltpu.VMEM((2, 4, BS, BS), f32), pltpu.VMEM((2, 2, 8, BS), f32),
-            pltpu.VMEM((2, 8, BS), jnp.int32), dma((2, 5)), dma((2,)),
-        ],
-        input_output_aliases={6: 2},
-        compiler_params=grant(58),
-    )(rhs, weights, aggregates, columns, fine_blocks.reshape(ROWS * 3 * BS, BS), smoother, mine)
     before = lax.ppermute(to_next, "gx", [(i, i + 1) for i in range(3)])
     after = lax.ppermute(to_previous, "gx", [(i + 1, i) for i in range(3)])
 
@@ -544,17 +543,17 @@
         edges_kernel,
         name="edges",
         out_shape=(shape(40, BS), shape(FEXT, BS), shape(ROWS, BS)),
-        in_specs=[HBM] * 3 + [SMEM] + [HBM] * 2 + [VMEM] * 3 + [HBM] * 2,
+        in_specs=[HBM] * 3 + [SMEM] + [HBM] * 2 + [VMEM] * 5,
         out_specs=(VMEM, VMEM, VMEM),
         scratch_shapes=[
-            pltpu.VMEM((2, 12, BS, BS), f32), pltpu.VMEM((2, 2, BS, BS), f32), pltpu.VMEM((2, HALO, BS), f32),
+            pltpu.VMEM((2, 12, BS, BS), f32), pltpu.VMEM((2, 2, BS, BS), f32),
             pltpu.VMEM((FEXT, BS), f32), pltpu.VMEM((2, 2, 8, BS), f32), pltpu.VMEM((2, 8, BS), jnp.int32),
-            pltpu.SMEM((2, 8, BS), f32), dma((2, 7)),
+            pltpu.SMEM((2, 8, BS), f32), dma((2, 6)),
         ],
-        compiler_params=grant(58),
+        compiler_params=grant(54),
     )(rhs, weights, aggregates, columns, fine, turned, first, second, total, before, after)
-    previous = lax.ppermute(mine, "gy", [(i, i + 1) for i in range(GROUPS - 1)])
-    following = lax.ppermute(mine, "gy", [(i + 1, i) for i in range(GROUPS - 1)])
+    previous = lax.ppermute(for_next, "gy", [(i, i + 1) for i in range(GROUPS - 1)])
+    following = lax.ppermute(for_previous, "gy", [(i + 1, i) for i in range(GROUPS - 1)])
     for bit in (1, 2):
         shared = shared + lax.ppermute(shared, "gx", [(i, i ^ bit) for i in range(4)])
 
@@ -580,7 +579,7 @@
             pltpu.VMEM((GROUPS + 2, 8, BS), f32),
             pltpu.VMEM((GROUPS + 8, BS), f32), pltpu.VMEM((GROUPS + 8, BS), f32), pltpu.VMEM((8, BS), f32),
             pltpu.VMEM((FEXT, BS), f32), pltpu.VMEM((FEXT, BS), f32), pltpu.SMEM((2, 8, BS), f32),
-            pltpu.VMEM((ROWS, BS), f32), pltpu.VMEM((ROWS, BS), jnp.int32), dma((11,)), dma((3, 4)), dma((4,)),
+            pltpu.VMEM((ROWS, BS), f32), pltpu.VMEM((ROWS, BS), jnp.int32), dma((12,)), dma((3, 4)), dma((4,)),
         ],
         compiler_params=grant(58),
     )(

time: 97.3 us -> 95.5 us (0.982)
    pallas_call x2 -> x1, Pallas kernels: 7.3 us -> 6.41 us  [per_device(): pl.pallas_call(prepare_kernel, name='prepare', out_shape=(shape(3, BS, BS...]
  transfers between devices with their start and end apart: 7 -> 7, of which waited for: 2 -> 2; matrix products, arithmetic and copies ran while one was open for 1% -> 1% of each run, Pallas kernels for 24% -> 22%
where the time goes in v2:
time: 95.5 us; the launch traced here: 95 us
  Pallas kernels  40.2 us (42%)
  blocking collectives  19.9 us (21%)
  starting transfers between devices  15.9 us (17%)
  between operations  14.2 us (15%)
  waiting for transfers between devices  3.15 us (3%)
  local copies, waits for them, and re-layouts  0.97 us (1%)
    all_to_all x1, blocking collectives, per_device(): parts = lax.all_to_all(spread, 'gy', 0, 0)  19.9 us
    pallas_call x1, Pallas kernels, per_device(): pl.pallas_call(interior_kernel, name='interior', out_shape=(shape(ROWS, B...  15.2 us
    pallas_call x1, Pallas kernels, per_device(): pl.pallas_call(correct_kernel, name='correct', out_shape=(shape(ROWS, BS)...  13.1 us
    pallas_call x1, Pallas kernels, per_device(): pl.pallas_call(prepare_kernel, name='prepare', out_shape=(shape(3, BS, BS...  6.41 us
    ppermute x2, starting transfers between devices, per_device(): lax.ppermute(shared, 'gx', [(i, i ^ bit) for i in range(4)])  4.86 us
    pallas_call x1, Pallas kernels, per_device(): pl.pallas_call(edges_kernel, name='edges', out_shape=(shape(40, BS), shap...  4.17 us
    ppermute x1, starting transfers between devices, per_device(): lax.ppermute(for_previous, 'gy', [(i + 1, i) for i in range(GROUPS - 1)])  3.33 us
    ppermute x1, starting transfers between devices, per_device(): before = lax.ppermute(to_next, 'gx', [(i, i + 1) for i in range(3)])  3.23 us
  transfers between devices with their start and end apart: 7, of which 2 were waited for; matrix products, arithmetic and copies ran while one was open for 1% of the time, Pallas kernels for 22%

profile of v2, /device:TPU:1, one launch (start us, length us, event | category | flops | bytes accessed | tf_op | source)
XLA Modules:
  0.0 95.0 jit_solution(16489328559826861877)
XLA Ops:
  7.2 0.0 all-gather.3.cloned.1.call-start
  7.2 6.4 %prepare.1 = (f32[3,128,128]{2,1,0:T(8,128)}, f32[18,128,128]{2,1,0:T(8,128)}, f32[14,128,128]{2,1,0:T(8,128)}, f32[12,128,128]{2,1,0:T(8,128)}, f32[1048,128]{1,0:T(8,128)}, /*index=5*/f32[1048,128]{1,0:T(8,128)}) custom-call(f32[4,128,128]{2,1,0:T(8,128)} %lower.1, f32[4,128,128]{2,1,0:T(8,128)} %upper.1, f32[4,128,128]{2,1,0:T(8,128)} %pivot.1, ...), custom_call_target="tpu_custom_call" | custom-call | tf_op jit(solution)/shard_map/prepare/pallas_call | solution.py:504
  13.6 0.0 all-gather.3.cloned.1.call-update
  13.7 3.3 %collective-permute-start.5 = (f32[14,128,128]{2,1,0:T(8,128)}, f32[14,128,128]{2,1,0:T(8,128)S(1)}, u32[]{:S(2)}, u32[]{:S(2)}) collective-permute-start(f32[14,128,128]{2,1,0:T(8,128)} %get-tuple-element.26), channel_id=1, source_target_pairs={{1,0},{2,1},{3,2},{4,3},{5,4},{6,5},{7,6},{8,7},{9,8},{10,9},{11,1... | collective-permute-start | bytes 2752520 | tf_op jit(solution)/shard_map/ppermute | solution.py:556
  17.0 3.1 %collective-permute-start.4 = (f32[12,128,128]{2,1,0:T(8,128)}, f32[12,128,128]{2,1,0:T(8,128)S(1)}, u32[]{:S(2)}, u32[]{:S(2)}) collective-permute-start(f32[12,128,128]{2,1,0:T(8,128)} %get-tuple-element.25), channel_id=1, source_target_pairs={{0,1},{1,2},{2,3},{3,4},{4,5},{5,6},{6,7},{7,8},{8,9},{9,10},{10,1... | collective-permute-start | bytes 2359304 | tf_op jit(solution)/shard_map/ppermute | solution.py:555
  20.1 3.2 %collective-permute-start = (f32[1048,128]{1,0:T(8,128)}, f32[1048,128]{1,0:T(8,128)S(1)}, u32[]{:S(2)}, u32[]{:S(2)}) collective-permute-start(f32[1048,128]{1,0:T(8,128)} %get-tuple-element.17.packed), channel_id=1, source_target_pairs={{0,32},{32,64},{64,96},{1,33},{33,65},{65,97},{2,34},{34,66},{66,9... | collective-permute-start | bytes 1609736 | tf_op jit(solution)/shard_map/ppermute | solution.py:524
  23.3 1.3 %collective-permute-start.1 = (f32[1048,128]{1,0:T(8,128)}, f32[1048,128]{1,0:T(8,128)S(1)}, u32[]{:S(2)}, u32[]{:S(2)}) collective-permute-start(f32[1048,128]{1,0:T(8,128)} %get-tuple-element.22), channel_id=1, source_target_pairs={{32,0},{64,32},{96,64},{33,1},{65,33},{97,65},{34,2},{66,34},{98,6... | collective-permute-start | bytes 1609736 | tf_op jit(solution)/shard_map/ppermute | solution.py:525
  24.6 15.2 %interior.1 = (f32[64,128,128]{2,1,0:T(8,128)}, f32[64,128]{1,0:T(8,128)}, f32[64,128]{1,0:T(8,128)}, f32[16,128]{1,0:T(8,128)}) custom-call(f32[64,128]{1,0:T(8,128)} %bitcast.25, f32[64,128]{1,0:T(8,128)} %bitcast.17, s32[64,128]{1,0:T(8,128)} %bitcast.21, s32[3,1,64]{2,1,0:T(1,128)} %bitcast.28, f32[192,128,128]{2,1,0:T(8,128)} %bitcast.10, ...), custom_call_target="tpu_custom_call" | custom-call | tf_op jit(solution)/shard_map/interior/pallas_call | solution.py:527
  39.9 0.0 collective-permute-done.before.before_hbm
  39.9 0.0 copy-start.4
  39.9 0.0 collective-permute-done.1.after.after_hbm
  39.9 0.0 copy-start.5
  39.9 0.8 copy-done.4
  40.7 0.2 copy-done.5
  40.9 0.0 copy-start
  40.9 4.2 %edges.1 = (f32[40,128]{1,0:T(8,128)}, f32[72,128]{1,0:T(8,128)}, f32[64,128]{1,0:T(8,128)}) custom-call(f32[64,128]{1,0:T(8,128)} %bitcast.26, f32[64,128]{1,0:T(8,128)} %bitcast.18, s32[64,128]{1,0:T(8,128)} %bitcast.22, s32[3,1,64]{2,1,0:T(1,128)} %bitcast.29, f32[192,128,128]{2,1,0:T(8,128)} %bitcast.11, f32[64,128,128]{2,1,0:T(8,128)} %get-tuple-element.18.turned_hbm, ...), custom_call_target="tpu_custom_call" | custom-call | tf_op jit(solution)/shard_map/edges/pallas_call | solution.py:542
  45.1 2.1 %collective-permute-start.2 = (f32[40,128]{1,0:T(8,128)}, f32[40,128]{1,0:T(8,128)S(1)}, u32[]{:S(2)}, u32[]{:S(2)}) collective-permute-start(f32[40,128]{1,0:T(8,128)} %get-tuple-element.23), channel_id=1, source_target_pairs={{0,32},{32,0},{64,96},{96,64},{1,33},{33,1},{65,97},{97,65},{2,34}... | collective-permute-start | bytes 61448 | tf_op jit(solution)/shard_map/ppermute | solution.py:558
  47.2 1.7 %collective-permute-done.2 = f32[40,128]{1,0:T(8,128)S(1)} collective-permute-done((f32[40,128]{1,0:T(8,128)}, f32[40,128]{1,0:T(8,128)S(1)}, u32[]{:S(2)}, u32[]{:S(2)}) %collective-permute-start.2) | collective-permute-done | bytes 20512 | tf_op jit(solution)/shard_map/ppermute | solution.py:558
  48.9 0.7 add.6
  49.6 2.7 %collective-permute-start.3 = (f32[40,128]{1,0:T(8,128)S(1)}, f32[40,128]{1,0:T(8,128)S(1)}, u32[]{:S(2)}, u32[]{:S(2)}) collective-permute-start(f32[40,128]{1,0:T(8,128)S(1)} %add.6), channel_id=1, source_target_pairs={{0,64},{32,96},{64,0},{96,32},{1,65},{33,97},{65,1},{97,33},{2,66}... | collective-permute-start | bytes 61448 | tf_op jit(solution)/shard_map/ppermute | solution.py:558
  52.4 1.4 %collective-permute-done.3 = f32[40,128]{1,0:T(8,128)S(1)} collective-permute-done((f32[40,128]{1,0:T(8,128)S(1)}, f32[40,128]{1,0:T(8,128)S(1)}, u32[]{:S(2)}, u32[]{:S(2)}) %collective-permute-start.3) | collective-permute-done | bytes 20512 | tf_op jit(solution)/shard_map/ppermute | solution.py:558
  53.8 0.0 copy-start.3
  53.8 0.0 collective-permute-done.4.previous
  53.8 0.0 copy-start.2
  53.8 0.0 collective-permute-done.5.following
  53.8 0.0 copy-start.1
  53.8 0.0 copy-done
  53.8 1.3 %local_solutions.1 = f32[32,24,128]{2,1,0:T(8,128)S(1)} custom-call(f32[40,128]{1,0:T(8,128)S(1)} %add.7.shared, f32[18,128,128]{2,1,0:T(8,128)S(1)} %copy-done, f32[12,128,128]{2,1,0:T(8,128)S(1)} %collective-permute-done.4.previous, f32[14,128,128]{2,1,0:T(8,128)S(1)} %collective-permute-done.5.following), custom_call_target="tpu_custom_call" | custom-call | tf_op jit(solution)/shard_map/local_solutions/pallas_call | solution.py:560
  55.2 19.9 %all_to_all.5.parts_hbm = f32[32,24,128]{2,1,0:T(8,128)} all-to-all(f32[32,24,128]{2,1,0:T(8,128)S(1)} %local_solutions.1), channel_id=1, replica_groups=mesh['gx'=4,'gy'=32] {'gy'}, dimensions={0} | all-to-all | bytes 786432 | tf_op jit(solution)/shard_map/all_to_all | solution.py:568
  75.0 0.0 all-gather.3.cloned.1.call-done
  75.0 0.0 copy-done.3
  75.0 0.0 copy-done.2
  75.0 0.0 copy-done.1
  75.0 13.1 %correct.1 = (f32[64,128]{1,0:T(8,128)}, f32[4,128]{1,0:T(4,128)}) custom-call(f32[32,24,128]{2,1,0:T(8,128)} %all_to_all.5.parts_hbm, f32[40,128]{1,0:T(8,128)} %copy-done.3, f32[72,128]{1,0:T(8,128)} %get-tuple-element.27.first_field, f32[64,128]{1,0:T(8,128)} %get-tuple-element.28.second_own, f32[64,128]{1,0:T(8,128)} %bitcast.19, s32[64,128]{1,0:T(8,128)} %bitcast.23, ...), custom_call_target="tpu_custom_call" | custom-call | tf_op jit(solution)/shard_map/correct/pallas_call | solution.py:570
  (1 shorter events, 0.0 us)
Async XLA Ops:
  7.2 67.9 %all-gather.3.cloned.1.call-start = ((), (), s32[]{:S(2)}) async-start(), calls=%async_computation.1 | async-start | bytes 6488064 | tf_op jit(solution)/shard_map/all_gather | solution.py:522
  13.7 40.2 %collective-permute-start.5 = (f32[14,128,128]{2,1,0:T(8,128)}, f32[14,128,128]{2,1,0:T(8,128)S(1)}, u32[]{:S(2)}, u32[]{:S(2)}) collective-permute-start(f32[14,128,128]{2,1,0:T(8,128)} %get-tuple-element.26), channel_id=1, source_target_pairs={{1,0},{2,1},{3,2},{4,3},{5,4},{6,5},{7,6},{8,7},{9,8},{10,9},{11,1... | collective-permute-start | bytes 2752520 | tf_op jit(solution)/shard_map/ppermute | solution.py:556
  17.0 36.8 %collective-permute-start.4 = (f32[12,128,128]{2,1,0:T(8,128)}, f32[12,128,128]{2,1,0:T(8,128)S(1)}, u32[]{:S(2)}, u32[]{:S(2)}) collective-permute-start(f32[12,128,128]{2,1,0:T(8,128)} %get-tuple-element.25), channel_id=1, source_target_pairs={{0,1},{1,2},{2,3},{3,4},{4,5},{5,6},{6,7},{7,8},{8,9},{9,10},{10,1... | collective-permute-start | bytes 2359304 | tf_op jit(solution)/shard_map/ppermute | solution.py:555
  20.1 19.8 %collective-permute-start = (f32[1048,128]{1,0:T(8,128)}, f32[1048,128]{1,0:T(8,128)S(1)}, u32[]{:S(2)}, u32[]{:S(2)}) collective-permute-start(f32[1048,128]{1,0:T(8,128)} %get-tuple-element.17.packed), channel_id=1, source_target_pairs={{0,32},{32,64},{64,96},{1,33},{33,65},{65,97},{2,34},{34,66},{66,9... | collective-permute-start | bytes 1609736 | tf_op jit(solution)/shard_map/ppermute | solution.py:524
  23.3 16.6 %collective-permute-start.1 = (f32[1048,128]{1,0:T(8,128)}, f32[1048,128]{1,0:T(8,128)S(1)}, u32[]{:S(2)}, u32[]{:S(2)}) collective-permute-start(f32[1048,128]{1,0:T(8,128)} %get-tuple-element.22), channel_id=1, source_target_pairs={{32,0},{64,32},{96,64},{33,1},{65,33},{97,65},{34,2},{66,34},{98,6... | collective-permute-start | bytes 1609736 | tf_op jit(solution)/shard_map/ppermute | solution.py:525
  39.9 0.8 copy-start.4
  39.9 1.0 %copy-start.5 = (f32[1048,128]{1,0:T(8,128)}, f32[1048,128]{1,0:T(8,128)S(1)}, u32[]{:S(2)}) copy-start(f32[1048,128]{1,0:T(8,128)S(1)} %collective-permute-done.1.after.after_hbm) | copy-start | bytes 1609732
  40.9 12.9 %copy-start = (f32[18,128,128]{2,1,0:T(8,128)S(1)}, f32[18,128,128]{2,1,0:T(8,128)}, u32[]{:S(2)}) copy-start(f32[18,128,128]{2,1,0:T(8,128)} %get-tuple-element.24.mine) | copy-start | bytes 3538948
  45.1 3.8 %collective-permute-start.2 = (f32[40,128]{1,0:T(8,128)}, f32[40,128]{1,0:T(8,128)S(1)}, u32[]{:S(2)}, u32[]{:S(2)}) collective-permute-start(f32[40,128]{1,0:T(8,128)} %get-tuple-element.23), channel_id=1, source_target_pairs={{0,32},{32,0},{64,96},{96,64},{1,33},{33,1},{65,97},{97,65},{2,34}... | collective-permute-start | bytes 61448 | tf_op jit(solution)/shard_map/ppermute | solution.py:558
  49.6 4.2 %collective-permute-start.3 = (f32[40,128]{1,0:T(8,128)S(1)}, f32[40,128]{1,0:T(8,128)S(1)}, u32[]{:S(2)}, u32[]{:S(2)}) collective-permute-start(f32[40,128]{1,0:T(8,128)S(1)} %add.6), channel_id=1, source_target_pairs={{0,64},{32,96},{64,0},{96,32},{1,65},{33,97},{65,1},{97,33},{2,66}... | collective-permute-start | bytes 61448 | tf_op jit(solution)/shard_map/ppermute | solution.py:558
  53.8 21.2 %copy-start.3 = (f32[40,128]{1,0:T(8,128)}, f32[40,128]{1,0:T(8,128)S(1)}, u32[]{:S(2)}) copy-start(f32[40,128]{1,0:T(8,128)S(1)} %add.7.shared) | copy-start | bytes 61444
  53.8 21.2 %copy-start.2 = (f32[12,128,128]{2,1,0:T(8,128)}, f32[12,128,128]{2,1,0:T(8,128)S(1)}, u32[]{:S(2)}) copy-start(f32[12,128,128]{2,1,0:T(8,128)S(1)} %collective-permute-done.4.previous) | copy-start | bytes 2359300
  53.8 21.2 %copy-start.1 = (f32[14,128,128]{2,1,0:T(8,128)}, f32[14,128,128]{2,1,0:T(8,128)S(1)}, u32[]{:S(2)}) copy-start(f32[14,128,128]{2,1,0:T(8,128)S(1)} %collective-permute-done.5.following) | copy-start | bytes 2752516
Sparse Core Ops, SparseCore 0:
  13.8 53.0 all-gather.2

commit v3 on v2

--- a/solution.py
+++ b/solution.py
@@ -205,38 +205,49 @@
         part = pl.ds(c * CHUNK, CHUNK)
         return pltpu.make_async_copy(turned.at[part], turned_out.at[part], out_sems.at[c])
 
-    for c in range(n_chunks):
+    ahead = 2
+    for c in range(ahead):
         fetch(c).start()
     for c in range(n_chunks):
+        if c + ahead < n_chunks:
+            fetch(c + ahead).start()
         block_copy(c).start()
     for action in small:
         action.wait()
 
-    def first_row(n, _):
+    def first_row(n):
         block = smooth[n]
-        column = jnp.sum(block * rows[0, pl.ds(n, 1)], axis=1, keepdims=True)
-        first[pl.ds(n, 1)] = column_to_row(column, eye)
         turned[n] = block.T
-        return 0
-
-    for c in range(n_chunks):
-        fetch(c).wait()
-        lax.fori_loop(c * CHUNK, c * CHUNK + CHUNK, first_row, 0, unroll=8)
-        store(c).start()
+        return column_to_row(jnp.sum(block * rows[0, n : n + 1], axis=1, keepdims=True), eye)
+
     base = gx * ROWS
 
     def picks(n):
         return [jnp.clip(columns[k, 0, n] - base, 0, ROWS - 1) for k in range(3)]
 
-    def second_row(n, _):
+    def second_row(n):
         change = change_row(own_blocks(blocks, n), turned[n], first, picks(n))
-        second[pl.ds(n, 1)] = 2.0 * first[pl.ds(n, 1)] - change
-        return 0
-
-    second[...] = jnp.zeros_like(second)
-    for c in range(n_chunks):
-        block_copy(c).wait()
-        lax.fori_loop(max(c * CHUNK, 2), min(c * CHUNK + CHUNK, ROWS - 2), second_row, 0, unroll=True)
+        return 2.0 * first[n : n + 1] - change
+
+    zero = jnp.zeros((1, BS), f32)
+    for c in range(-ahead, n_chunks):
+        new, old = c + ahead, c
+        if new < n_chunks:
+            fetch(new).wait()
+        if old >= 0:
+            block_copy(old).wait()
+        found, done = [], []
+        for r in range(CHUNK):
+            if new < n_chunks:
+                found.append(first_row(new * CHUNK + r))
+            if old >= 0:
+                n = old * CHUNK + r
+                done.append(second_row(n) if 2 <= n < ROWS - 2 else zero)
+        if found:
+            first[new * CHUNK : new * CHUNK + CHUNK] = jnp.concatenate(found, axis=0)
+            store(new).start()
+        if done:
+            second[old * CHUNK : old * CHUNK + CHUNK] = jnp.concatenate(done, axis=0)
 
     def residual_row(n, _):
         column = change_row(own_blocks(blocks, n), None, second, picks(n))

time: 95.5 us -> 94.9 us (level)
  transfers between devices with their start and end apart: 7 -> 7, of which waited for: 2 -> 3; matrix products, arithmetic and copies ran while one was open for 1% -> 1% of each run, Pallas kernels for 22% -> 21%
where the time goes in v3:
time: 94.9 us; the launch traced here: 94.4 us
  Pallas kernels  39.6 us (42%)
  blocking collectives  20.1 us (21%)
  starting transfers between devices  16.1 us (17%)
  between operations  14.2 us (15%)
  waiting for transfers between devices  2.86 us (3%)
    all_to_all x1, blocking collectives, per_device(): parts = lax.all_to_all(spread, 'gy', 0, 0)  20.1 us
    pallas_call x1, Pallas kernels, per_device(): pl.pallas_call(interior_kernel, name='interior', out_shape=(shape(ROWS, B...  14.7 us
    pallas_call x1, Pallas kernels, per_device(): pl.pallas_call(correct_kernel, name='correct', out_shape=(shape(ROWS, BS)...  13.1 us
    pallas_call x1, Pallas kernels, per_device(): pl.pallas_call(prepare_kernel, name='prepare', out_shape=(shape(3, BS, BS...  6.42 us
    ppermute x2, starting transfers between devices, per_device(): lax.ppermute(shared, 'gx', [(i, i ^ bit) for i in range(4)])  5.1 us
    pallas_call x1, Pallas kernels, per_device(): pl.pallas_call(edges_kernel, name='edges', out_shape=(shape(40, BS), shap...  4.17 us
    ppermute x1, starting transfers between devices, per_device(): lax.ppermute(for_previous, 'gy', [(i + 1, i) for i in range(GROUPS - 1)])  3.33 us
    ppermute x1, starting transfers between devices, per_device(): before = lax.ppermute(to_next, 'gx', [(i, i + 1) for i in range(3)])  3.23 us
  transfers between devices with their start and end apart: 7, of which 3 were waited for; matrix products, arithmetic and copies ran while one was open for 1% of the time, Pallas kernels for 21%

profile of v3, /device:TPU:1, one launch (start us, length us, event | category | flops | bytes accessed | tf_op | source)
XLA Modules:
  0.0 94.4 jit_solution(14477365250214666581)
XLA Ops:
  7.2 0.0 all-gather.3.cloned.1.call-start
  7.2 6.4 %prepare.1 = (f32[3,128,128]{2,1,0:T(8,128)}, f32[18,128,128]{2,1,0:T(8,128)}, f32[14,128,128]{2,1,0:T(8,128)}, f32[12,128,128]{2,1,0:T(8,128)}, f32[1048,128]{1,0:T(8,128)}, /*index=5*/f32[1048,128]{1,0:T(8,128)}) custom-call(f32[4,128,128]{2,1,0:T(8,128)} %lower.1, f32[4,128,128]{2,1,0:T(8,128)} %upper.1, f32[4,128,128]{2,1,0:T(8,128)} %pivot.1, ...), custom_call_target="tpu_custom_call" | custom-call | tf_op jit(solution)/shard_map/prepare/pallas_call | solution.py:515
  13.6 0.0 all-gather.3.cloned.1.call-update
  13.7 3.3 %collective-permute-start.5 = (f32[14,128,128]{2,1,0:T(8,128)}, f32[14,128,128]{2,1,0:T(8,128)S(1)}, u32[]{:S(2)}, u32[]{:S(2)}) collective-permute-start(f32[14,128,128]{2,1,0:T(8,128)} %get-tuple-element.26), channel_id=1, source_target_pairs={{1,0},{2,1},{3,2},{4,3},{5,4},{6,5},{7,6},{8,7},{9,8},{10,9},{11,1... | collective-permute-start | bytes 2752520 | tf_op jit(solution)/shard_map/ppermute | solution.py:567
  17.0 3.1 %collective-permute-start.4 = (f32[12,128,128]{2,1,0:T(8,128)}, f32[12,128,128]{2,1,0:T(8,128)S(1)}, u32[]{:S(2)}, u32[]{:S(2)}) collective-permute-start(f32[12,128,128]{2,1,0:T(8,128)} %get-tuple-element.25), channel_id=1, source_target_pairs={{0,1},{1,2},{2,3},{3,4},{4,5},{5,6},{6,7},{7,8},{8,9},{9,10},{10,1... | collective-permute-start | bytes 2359304 | tf_op jit(solution)/shard_map/ppermute | solution.py:566
  20.1 3.2 %collective-permute-start = (f32[1048,128]{1,0:T(8,128)}, f32[1048,128]{1,0:T(8,128)S(1)}, u32[]{:S(2)}, u32[]{:S(2)}) collective-permute-start(f32[1048,128]{1,0:T(8,128)} %get-tuple-element.17.packed), channel_id=1, source_target_pairs={{0,32},{32,64},{64,96},{1,33},{33,65},{65,97},{2,34},{34,66},{66,9... | collective-permute-start | bytes 1609736 | tf_op jit(solution)/shard_map/ppermute | solution.py:535
  23.3 1.3 %collective-permute-start.1 = (f32[1048,128]{1,0:T(8,128)}, f32[1048,128]{1,0:T(8,128)S(1)}, u32[]{:S(2)}, u32[]{:S(2)}) collective-permute-start(f32[1048,128]{1,0:T(8,128)} %get-tuple-element.22), channel_id=1, source_target_pairs={{32,0},{64,32},{96,64},{33,1},{65,33},{97,65},{34,2},{66,34},{98,6... | collective-permute-start | bytes 1609736 | tf_op jit(solution)/shard_map/ppermute | solution.py:536
  24.6 14.7 %interior.1 = (f32[64,128,128]{2,1,0:T(8,128)}, f32[64,128]{1,0:T(8,128)}, f32[64,128]{1,0:T(8,128)}, f32[16,128]{1,0:T(8,128)}) custom-call(f32[64,128]{1,0:T(8,128)} %bitcast.25, f32[64,128]{1,0:T(8,128)} %bitcast.17, s32[64,128]{1,0:T(8,128)} %bitcast.21, s32[3,1,64]{2,1,0:T(1,128)} %bitcast.28, f32[192,128,128]{2,1,0:T(8,128)} %bitcast.10, ...), custom_call_target="tpu_custom_call" | custom-call | tf_op jit(solution)/shard_map/interior/pallas_call | solution.py:538
  39.3 0.0 collective-permute-done.before.before_hbm
  39.3 0.0 copy-start.4
  39.3 0.2 collective-permute-done.1.after.after_hbm
  39.6 0.0 copy-start.5
  39.6 0.5 copy-done.4
  40.1 0.3 copy-done.5
  40.4 0.0 copy-start
  40.4 4.2 %edges.1 = (f32[40,128]{1,0:T(8,128)}, f32[72,128]{1,0:T(8,128)}, f32[64,128]{1,0:T(8,128)}) custom-call(f32[64,128]{1,0:T(8,128)} %bitcast.26, f32[64,128]{1,0:T(8,128)} %bitcast.18, s32[64,128]{1,0:T(8,128)} %bitcast.22, s32[3,1,64]{2,1,0:T(1,128)} %bitcast.29, f32[192,128,128]{2,1,0:T(8,128)} %bitcast.11, f32[64,128,128]{2,1,0:T(8,128)} %get-tuple-element.18.turned_hbm, ...), custom_call_target="tpu_custom_call" | custom-call | tf_op jit(solution)/shard_map/edges/pallas_call | solution.py:553
  44.5 2.1 %collective-permute-start.2 = (f32[40,128]{1,0:T(8,128)}, f32[40,128]{1,0:T(8,128)S(1)}, u32[]{:S(2)}, u32[]{:S(2)}) collective-permute-start(f32[40,128]{1,0:T(8,128)} %get-tuple-element.23), channel_id=1, source_target_pairs={{0,32},{32,0},{64,96},{96,64},{1,33},{33,1},{65,97},{97,65},{2,34}... | collective-permute-start | bytes 61448 | tf_op jit(solution)/shard_map/ppermute | solution.py:569
  46.6 1.4 %collective-permute-done.2 = f32[40,128]{1,0:T(8,128)S(1)} collective-permute-done((f32[40,128]{1,0:T(8,128)}, f32[40,128]{1,0:T(8,128)S(1)}, u32[]{:S(2)}, u32[]{:S(2)}) %collective-permute-start.2) | collective-permute-done | bytes 20512 | tf_op jit(solution)/shard_map/ppermute | solution.py:569
  48.0 0.7 add.6
  48.7 3.0 %collective-permute-start.3 = (f32[40,128]{1,0:T(8,128)S(1)}, f32[40,128]{1,0:T(8,128)S(1)}, u32[]{:S(2)}, u32[]{:S(2)}) collective-permute-start(f32[40,128]{1,0:T(8,128)S(1)} %add.6), channel_id=1, source_target_pairs={{0,64},{32,96},{64,0},{96,32},{1,65},{33,97},{65,1},{97,33},{2,66}... | collective-permute-start | bytes 61448 | tf_op jit(solution)/shard_map/ppermute | solution.py:569
  51.8 1.2 %collective-permute-done.3 = f32[40,128]{1,0:T(8,128)S(1)} collective-permute-done((f32[40,128]{1,0:T(8,128)S(1)}, f32[40,128]{1,0:T(8,128)S(1)}, u32[]{:S(2)}, u32[]{:S(2)}) %collective-permute-start.3) | collective-permute-done | bytes 20512 | tf_op jit(solution)/shard_map/ppermute | solution.py:569
  53.0 0.0 copy-start.3
  53.0 0.0 collective-permute-done.4.previous
  53.0 0.0 copy-start.2
  53.0 0.0 collective-permute-done.5.following
  53.0 0.0 copy-start.1
  53.0 0.0 copy-done
  53.0 1.3 %local_solutions.1 = f32[32,24,128]{2,1,0:T(8,128)S(1)} custom-call(f32[40,128]{1,0:T(8,128)S(1)} %add.7.shared, f32[18,128,128]{2,1,0:T(8,128)S(1)} %copy-done, f32[12,128,128]{2,1,0:T(8,128)S(1)} %collective-permute-done.4.previous, f32[14,128,128]{2,1,0:T(8,128)S(1)} %collective-permute-done.5.following), custom_call_target="tpu_custom_call" | custom-call | tf_op jit(solution)/shard_map/local_solutions/pallas_call | solution.py:571
  54.3 20.1 %all_to_all.5.parts_hbm = f32[32,24,128]{2,1,0:T(8,128)} all-to-all(f32[32,24,128]{2,1,0:T(8,128)S(1)} %local_solutions.1), channel_id=1, replica_groups=mesh['gx'=4,'gy'=32] {'gy'}, dimensions={0} | all-to-all | bytes 786432 | tf_op jit(solution)/shard_map/all_to_all | solution.py:579
  74.4 0.0 all-gather.3.cloned.1.call-done
  74.5 0.0 copy-done.3
  74.5 0.0 copy-done.2
  74.5 0.0 copy-done.1
  74.5 13.1 %correct.1 = (f32[64,128]{1,0:T(8,128)}, f32[4,128]{1,0:T(4,128)}) custom-call(f32[32,24,128]{2,1,0:T(8,128)} %all_to_all.5.parts_hbm, f32[40,128]{1,0:T(8,128)} %copy-done.3, f32[72,128]{1,0:T(8,128)} %get-tuple-element.27.first_field, f32[64,128]{1,0:T(8,128)} %get-tuple-element.28.second_own, f32[64,128]{1,0:T(8,128)} %bitcast.19, s32[64,128]{1,0:T(8,128)} %bitcast.23, ...), custom_call_target="tpu_custom_call" | custom-call | tf_op jit(solution)/shard_map/correct/pallas_call | solution.py:581
  (1 shorter events, 0.0 us)
Async XLA Ops:
  7.2 67.3 %all-gather.3.cloned.1.call-start = ((), (), s32[]{:S(2)}) async-start(), calls=%async_computation.1 | async-start | bytes 6488064 | tf_op jit(solution)/shard_map/all_gather | solution.py:533
  13.7 39.3 %collective-permute-start.5 = (f32[14,128,128]{2,1,0:T(8,128)}, f32[14,128,128]{2,1,0:T(8,128)S(1)}, u32[]{:S(2)}, u32[]{:S(2)}) collective-permute-start(f32[14,128,128]{2,1,0:T(8,128)} %get-tuple-element.26), channel_id=1, source_target_pairs={{1,0},{2,1},{3,2},{4,3},{5,4},{6,5},{7,6},{8,7},{9,8},{10,9},{11,1... | collective-permute-start | bytes 2752520 | tf_op jit(solution)/shard_map/ppermute | solution.py:567
  17.0 36.0 %collective-permute-start.4 = (f32[12,128,128]{2,1,0:T(8,128)}, f32[12,128,128]{2,1,0:T(8,128)S(1)}, u32[]{:S(2)}, u32[]{:S(2)}) collective-permute-start(f32[12,128,128]{2,1,0:T(8,128)} %get-tuple-element.25), channel_id=1, source_target_pairs={{0,1},{1,2},{2,3},{3,4},{4,5},{5,6},{6,7},{7,8},{8,9},{9,10},{10,1... | collective-permute-start | bytes 2359304 | tf_op jit(solution)/shard_map/ppermute | solution.py:566
  20.1 19.2 %collective-permute-start = (f32[1048,128]{1,0:T(8,128)}, f32[1048,128]{1,0:T(8,128)S(1)}, u32[]{:S(2)}, u32[]{:S(2)}) collective-permute-start(f32[1048,128]{1,0:T(8,128)} %get-tuple-element.17.packed), channel_id=1, source_target_pairs={{0,32},{32,64},{64,96},{1,33},{33,65},{65,97},{2,34},{34,66},{66,9... | collective-permute-start | bytes 1609736 | tf_op jit(solution)/shard_map/ppermute | solution.py:535
  23.3 16.2 %collective-permute-start.1 = (f32[1048,128]{1,0:T(8,128)}, f32[1048,128]{1,0:T(8,128)S(1)}, u32[]{:S(2)}, u32[]{:S(2)}) collective-permute-start(f32[1048,128]{1,0:T(8,128)} %get-tuple-element.22), channel_id=1, source_target_pairs={{32,0},{64,32},{96,64},{33,1},{65,33},{97,65},{34,2},{66,34},{98,6... | collective-permute-start | bytes 1609736 | tf_op jit(solution)/shard_map/ppermute | solution.py:536
  39.3 0.8 copy-start.4
  39.6 0.8 copy-start.5
  40.4 12.7 %copy-start = (f32[18,128,128]{2,1,0:T(8,128)S(1)}, f32[18,128,128]{2,1,0:T(8,128)}, u32[]{:S(2)}) copy-start(f32[18,128,128]{2,1,0:T(8,128)} %get-tuple-element.24.mine) | copy-start | bytes 3538948
  44.5 3.4 %collective-permute-start.2 = (f32[40,128]{1,0:T(8,128)}, f32[40,128]{1,0:T(8,128)S(1)}, u32[]{:S(2)}, u32[]{:S(2)}) collective-permute-start(f32[40,128]{1,0:T(8,128)} %get-tuple-element.23), channel_id=1, source_target_pairs={{0,32},{32,0},{64,96},{96,64},{1,33},{33,1},{65,97},{97,65},{2,34}... | collective-permute-start | bytes 61448 | tf_op jit(solution)/shard_map/ppermute | solution.py:569
  48.7 4.3 %collective-permute-start.3 = (f32[40,128]{1,0:T(8,128)S(1)}, f32[40,128]{1,0:T(8,128)S(1)}, u32[]{:S(2)}, u32[]{:S(2)}) collective-permute-start(f32[40,128]{1,0:T(8,128)S(1)} %add.6), channel_id=1, source_target_pairs={{0,64},{32,96},{64,0},{96,32},{1,65},{33,97},{65,1},{97,33},{2,66}... | collective-permute-start | bytes 61448 | tf_op jit(solution)/shard_map/ppermute | solution.py:569
  53.0 21.5 %copy-start.3 = (f32[40,128]{1,0:T(8,128)}, f32[40,128]{1,0:T(8,128)S(1)}, u32[]{:S(2)}) copy-start(f32[40,128]{1,0:T(8,128)S(1)} %add.7.shared) | copy-start | bytes 61444
  53.0 21.5 %copy-start.2 = (f32[12,128,128]{2,1,0:T(8,128)}, f32[12,128,128]{2,1,0:T(8,128)S(1)}, u32[]{:S(2)}) copy-start(f32[12,128,128]{2,1,0:T(8,128)S(1)} %collective-permute-done.4.previous) | copy-start | bytes 2359300
  53.0 21.4 %copy-start.1 = (f32[14,128,128]{2,1,0:T(8,128)}, f32[14,128,128]{2,1,0:T(8,128)S(1)}, u32[]{:S(2)}) copy-start(f32[14,128,128]{2,1,0:T(8,128)S(1)} %collective-permute-done.5.following) | copy-start | bytes 2752516
Sparse Core Ops, SparseCore 0:
  13.8 53.1 all-gather.2
